TPU v7x, 256 devices: a whole 4x4x8 slice. The times are simulated.
256 devices in a mesh: src: 8 (over z), dst: 32 (over x, y, core).
Axes of the slice: x: 4, y: 4, z: 8, core: 2. Of those that a mesh axis runs over, the one named last changes fastest.
Arguments:
- src_emb: bfloat16 [65536, 128], P('src'), may hold values from -1.5 to 1.5
- dst_emb: bfloat16 [65536, 128], P('dst'), may hold values from -1.5 to 1.5
- out_emb: bfloat16 [65536, 128], P('dst'), may hold values from -1.5 to 1.5
- word_table: bfloat16 [32768, 128], P('dst'), may hold values from -1.5 to 1.5
- log_norm: float32 [65536], P('dst'), may hold values from 9 to 11
- block_mask: int32 [128, 128], P('src', 'dst'), may hold values from 0 to 1, as said below
- tokens: int32 [3, 8], replicated, may hold values from 0 to 32767
- alpha_start: float32 [8, 65536], P(None, 'src'), may hold values from 0.5 to 80
- beta_end: float32 [8, 65536], P(None, 'dst'), may hold values from 0.5 to 80
Outputs:
- alpha_end: float32 [8, 65536], P(None, 'dst')
- beta_start: float32 [8, 65536], P(None, 'src')
- block_counts: float32 [128, 128], P('src', 'dst')
Inputs may be any that keep to these rules, and one draw needn't show every extreme that they name: block_mask[I, I] = 1 for every block I: a state may always move within its own block.
All inputs are finite; a program needn't handle non-finite values.
Results may differ from a plain program's by a relative error of at most 0.0032.
Values may be sent and summed in bfloat16 or wider, within the bound.
No kernel may reach another device: no remote copies, remote signals or barrier semaphores. Data moves between devices by JAX's collectives and lax.ppermute only.
A program may use at most 128 MiB of HBM per device.

v0:
```python
import jax
import jax.numpy as jnp
from jax import lax
from jax.sharding import PartitionSpec as P

BLK = 512
STEPS = 3
NB = 128


very_negative = -1e30


def local(
    src_emb, dst_emb, out_emb, word_table, log_norm, block_mask, tokens, alpha_start, beta_end
):
    row_count = src_emb.shape[0]
    col_count = dst_emb.shape[0]
    emb_width = src_emb.shape[1]
    row_blocks = row_count // BLK
    col_blocks = col_count // BLK
    traces = alpha_start.shape[0]
    src_count = lax.axis_size("src")
    states = row_count * src_count
    src_place = lax.axis_index("src")
    dst_place = lax.axis_index("dst")
    vocab_slice = word_table.shape[0]
    local_ids = tokens.reshape(-1) - dst_place * vocab_slice
    onehot = (local_ids[:, None] == jnp.arange(vocab_slice, dtype=jnp.int32)[None, :]).astype(
        jnp.bfloat16
    )
    looked = jnp.dot(onehot, word_table, preferred_element_type=jnp.float32)
    word_rows = lax.psum(looked.astype(jnp.bfloat16), "dst")
    logits = lax.dot_general(
        word_rows, out_emb, (((1,), (1,)), ((), ())), preferred_element_type=jnp.float32
    )
    emission = jnp.exp(logits - log_norm[None, :]).reshape(STEPS, traces, col_count)

    def table_block(running, inputs):
        src_rows, mask_row = inputs
        scores = lax.dot_general(
            src_rows, dst_emb, (((1,), (1,)), ((), ())), preferred_element_type=jnp.float32
        )
        scores = scores.reshape(BLK, col_blocks, BLK)
        block_top = jnp.max(scores, axis=2)
        block_sum = jnp.sum(jnp.exp(scores - block_top[:, :, None]), axis=2)
        allowed = (mask_row == 1)[None, :]
        row_best = jnp.max(jnp.where(allowed, block_top, very_negative), axis=1)
        row_mass = jnp.sum(
            jnp.where(allowed, block_sum * jnp.exp(block_top - row_best[:, None]), 0.0), axis=1
        )
        transit = jnp.where(
            allowed[:, :, None], jnp.exp(scores - block_top[:, :, None]), 0.0
        ).astype(jnp.bfloat16)
        return (running, (block_top.T, row_best, row_mass, transit))

    _, (block_top, row_best, row_mass, transit) = lax.scan(
        table_block, 0, (src_emb.reshape(row_blocks, BLK, emb_width), block_mask)
    )
    row_best = row_best.reshape(row_count)
    row_mass = row_mass.reshape(row_count)
    whole_best = lax.pmax(row_best, "dst")
    whole_mass = lax.psum(row_mass * jnp.exp(row_best - whole_best), "dst")
    log_total = (whole_best + jnp.log(whole_mass)).reshape(row_blocks, 1, BLK)
    factor = jnp.where(block_mask[:, :, None] == 1, jnp.exp(block_top - log_total), 0.0)

    def forward_finish(partial_value, scale, position, final):
        predicted = lax.psum(partial_value, "src")
        alpha_cols = predicted * emission[position] / scale[:, None]
        if final:
            return (alpha_cols, alpha_cols)
        gathered = lax.all_gather(alpha_cols, "dst", axis=1, tiled=True)
        alpha_rows = lax.dynamic_slice_in_dim(gathered, src_place * row_count, row_count, 1)
        return (alpha_rows, alpha_cols)

    def backward_finish(partial_value, scale, final):
        beta_rows = lax.psum(partial_value, "dst") / scale[:, None]
        if final:
            return (beta_rows, beta_rows)
        gathered = lax.all_gather(beta_rows, "src", axis=1, tiled=True)
        beta_cols = lax.dynamic_slice_in_dim(gathered, dst_place * col_count, col_count, 1)
        return (beta_rows, beta_cols)

    mix_store = [None] * STEPS
    spread_store = [None] * STEPS
    alpha_rows = alpha_start
    alpha_cols = None
    beta_rows = None
    beta_cols = beta_end
    for k in range(STEPS):
        mix_terms = (alpha_rows.reshape(traces, row_blocks, 1, BLK) * factor[None]).astype(
            jnp.bfloat16
        )
        forward_partial_value = jnp.einsum(
            "bijr,irjc->bjc", mix_terms, transit, preferred_element_type=jnp.float32
        )
        forward_partial_value = forward_partial_value.reshape(traces, col_count)
        mix_terms, forward_partial, forward_scale = (
            mix_terms,
            forward_partial_value,
            jnp.sum(forward_partial_value * emission[k], axis=1),
        )
        mix_store[k] = mix_terms
        forward_total = lax.psum(forward_scale, ("src", "dst"))
        alpha_rows, alpha_cols = forward_finish(
            forward_partial, forward_total / states, k, k == STEPS - 1
        )
    for k in range(STEPS):
        mirror = STEPS - 1 - k
        weights = (
            (emission[mirror] * beta_cols).astype(jnp.bfloat16).reshape(traces, col_blocks, BLK)
        )
        spread = jnp.einsum("irjc,bjc->bijr", transit, weights, preferred_element_type=jnp.float32)
        backward_partial_value = jnp.sum(factor[None] * spread, axis=2).reshape(traces, row_count)
        spread, backward_partial, backward_scale = (
            spread,
            backward_partial_value,
            jnp.sum(backward_partial_value, axis=1),
        )
        spread_store[mirror] = spread
        backward_total = lax.psum(backward_scale, ("src", "dst"))
        beta_rows, beta_cols = backward_finish(
            backward_partial, backward_total / states, mirror == 0
        )
    block_terms = jnp.stack(
        [jnp.sum(mix_store[t].astype(jnp.float32) * spread_store[t], axis=3) for t in range(STEPS)]
    )
    pair_total = lax.psum(jnp.sum(block_terms, axis=(2, 3)), ("src", "dst"))
    counts = jnp.sum(block_terms / pair_total[:, :, None, None], axis=(0, 1)) * (
        NB * NB / (STEPS * traces)
    )
    return (alpha_cols, beta_rows, counts)


def solution(mesh):
    return jax.shard_map(
        local,
        mesh=mesh,
        in_specs=(
            P("src", None),
            P("dst", None),
            P("dst", None),
            P("dst", None),
            P("dst"),
            P("src", "dst"),
            P(),
            P(None, "src"),
            P(None, "dst"),
        ),
        out_specs=(P(None, "dst"), P(None, "src"), P("src", "dst")),
        check_vma=False,
    )
```

profile of v0, /device:TPU:31, one launch (start us, length us, event | category | flops | bytes accessed | tf_op | source)
XLA Modules:
  0.0 1439.2 jit_solution(10150107876679491098)
XLA Ops:
  8.7 76.6 %while.17 = (s32[]{:T(128)}, f32[16,4,512]{2,1,0:T(4,128)S(1)}, f32[16,512]{1,0:T(8,128)S(1)}, f32[16,512]{1,0:T(8,128)S(1)}, bf16[16,512,4,512]{1,3,2,0:T(8,128...) while((s32[]{:T(128)}, f32[16,4,512]{2,1,0:T(4,128)S(1)}, ...), condition=%wide.region_5.6_spmd.clone, body=%wide.region_0.5_spmd.sunk.clone | while | flops 274734080 | bytes 15424645 | solution.py:57
  8.7 1.9 fusion.51
  10.6 2.0 fusion.53
  15.4 2.0 fusion.53
  18.3 1.8 fusion.51
  20.2 2.0 fusion.53
  23.1 1.8 fusion.51
  25.0 2.0 fusion.53
  29.8 2.1 fusion.53
  34.6 2.0 fusion.53
  39.3 2.1 fusion.53
  42.3 1.8 fusion.51
  44.2 2.0 fusion.53
  47.1 1.8 fusion.51
  48.9 2.0 fusion.53
  53.7 2.0 fusion.53
  56.6 1.8 fusion.51
  58.5 2.0 fusion.53
  61.4 1.8 fusion.51
  63.3 2.0 fusion.53
  68.1 2.1 fusion.53
  71.0 1.8 fusion.51
  72.9 2.0 fusion.53
  77.6 2.1 fusion.53
  80.6 1.8 fusion.51
  82.4 2.0 fusion.53
  85.4 123.2 %pmax.7 = f32[8192]{0:T(1024)S(1)} all-reduce(f32[8192]{0:T(1024)S(1)} %bitcast.119), channel_id=1, replica_groups=mesh['src'=8,'dst'=32] {'dst'}, use_global_device_ids=true, to_apply=%region_6.7 | all-reduce | flops 8192 | bytes 65536 | tf_op jit(solution)/shard_map/pmax | solution.py:62
  208.6 123.8 %psum.105 = f32[8192]{0:T(1024)S(1)} all-reduce(f32[8192]{0:T(1024)S(1)} %exponential_multiply_fusion), channel_id=1, replica_groups=mesh['src'=8,'dst'=32] {'dst'}, use_global_device_ids=true, to_apply=%region_7.8 | all-reduce | flops 8192 | bytes 65536 | tf_op jit(solution)/shard_map/psum | solution.py:63
  333.0 63.7 %psum.107 = bf16[24,128]{1,0:T(8,128)(2,1)S(1)} all-reduce(bf16[24,128]{1,0:T(8,128)(2,1)S(1)} %convolution_convert_fusion), channel_id=1, replica_groups=mesh['src'=8,'dst'=32] {'dst'}, use_global_device_ids=true, to_apply=%region_9.10 | all-reduce | flops 3072 | bytes 12288 | tf_op jit(solution)/shard_map/psum | solution.py:33
  396.7 13.9 fusion.27
  412.0 78.6 %psum.108 = f32[8]{0:T(128)S(1)} all-reduce(f32[8]{0:T(128)S(1)} %get-tuple-element.102), channel_id=1, replica_groups=mesh['src'=8,'dst'=32] {'src','dst'}, use_global_device_ids=true, to_apply=%region_11.12 | all-reduce | flops 8 | bytes 64 | tf_op jit(solution)/shard_map/psum | solution.py:104
  492.2 45.9 %all-gather.5.cloned.1.call-done = f32[8,65536]{1,0:T(8,128)} async-done(((f32[8,2048]{1,0:T(8,128)}), f32[8,65536]{1,0:T(8,128)}) %all-gather.5.cloned.1.call-update) | async-done | bytes 2097168 | tf_op jit(solution)/shard_map/all_gather | solution.py:72
  539.1 13.9 fusion.25
  553.2 74.6 %psum.110 = f32[8]{0:T(128)S(1)} all-reduce(f32[8]{0:T(128)S(1)} %multiply_reduce_fusion.10), channel_id=1, replica_groups=mesh['src'=8,'dst'=32] {'src','dst'}, use_global_device_ids=true, to_apply=%region_14.15 | all-reduce | flops 8 | bytes 64 | tf_op jit(solution)/shard_map/psum | solution.py:104
  627.9 66.4 %all-reduce.10.cloned.1.call-done = f32[8,2048]{1,0:T(8,128)} async-done(((f32[8,2048]{1,0:T(8,128)}), f32[8,2048]{1,0:T(8,128)}) %all-reduce.10.cloned.1.call-update) | async-done | bytes 65552 | tf_op jit(solution)/shard_map/psum | solution.py:68
  695.9 51.9 %all-gather.7.cloned.1.call-done = f32[8,65536]{1,0:T(8,128)} async-done(((f32[8,2048]{1,0:T(8,128)}), f32[8,65536]{1,0:T(8,128)}) %all-gather.7.cloned.1.call-update) | async-done | bytes 2097168 | tf_op jit(solution)/shard_map/all_gather | solution.py:72
  748.8 13.9 multiply_reduce_fusion
  762.7 74.5 %psum.114 = f32[8]{0:T(128)S(1)} all-reduce(f32[8]{0:T(128)S(1)} %get-tuple-element.75), channel_id=1, replica_groups=mesh['src'=8,'dst'=32] {'src','dst'}, use_global_device_ids=true, to_apply=%region_21.22 | all-reduce | flops 8 | bytes 64 | tf_op jit(solution)/shard_map/psum | solution.py:121
  837.3 110.5 %all-reduce.14.cloned.1.call-done = f32[8,8192]{1,0:T(8,128)} async-done(((f32[8,8192]{1,0:T(8,128)}), f32[8,8192]{1,0:T(8,128)}) %all-reduce.14.cloned.1.call-update) | async-done | bytes 262160 | tf_op jit(solution)/shard_map/psum | solution.py:77
  949.8 38.5 %all-gather.9.cloned.1.call-done = f32[8,65536]{1,0:T(8,128)} async-done(((f32[8,8192]{1,0:T(8,128)}), f32[8,65536]{1,0:T(8,128)}) %all-gather.9.cloned.1.call-update) | async-done | bytes 2097168 | tf_op jit(solution)/shard_map/all_gather | solution.py:80
  989.2 13.9 multiply_reduce_fusion.1
  1003.1 75.3 %psum.116 = f32[8]{0:T(128)S(1)} all-reduce(f32[8]{0:T(128)S(1)} %get-tuple-element.72), channel_id=1, replica_groups=mesh['src'=8,'dst'=32] {'src','dst'}, use_global_device_ids=true, to_apply=%region_25.26 | all-reduce | flops 8 | bytes 64 | tf_op jit(solution)/shard_map/psum | solution.py:121
  1078.4 109.7 %all-reduce.16.cloned.1.call-done = f32[8,8192]{1,0:T(8,128)} async-done(((f32[8,8192]{1,0:T(8,128)}), f32[8,8192]{1,0:T(8,128)}) %all-reduce.16.cloned.1.call-update) | async-done | bytes 262160 | tf_op jit(solution)/shard_map/psum | solution.py:77
  1190.0 13.9 fusion.23
  1204.0 24.7 %all-gather.11.cloned.1.call-done = f32[8,65536]{1,0:T(8,128)} async-done(((f32[8,8192]{1,0:T(8,128)}), f32[8,65536]{1,0:T(8,128)}) %all-gather.11.cloned.1.call-update) | async-done | bytes 2097168 | tf_op jit(solution)/shard_map/all_gather | solution.py:80
  1230.4 13.9 multiply_reduce_fusion.2
  1244.5 75.4 %all-reduce = (f32[8]{0:T(128)S(1)}, f32[8]{0:T(128)S(1)}, f32[3,8]{1,0:T(4,128)S(1)}) all-reduce(f32[8]{0:T(128)S(1)} %get-tuple-element.100, f32[8]{0:T(128)S(1)} %get-tuple-element.69, f32[3,8]{1,0:T(4,128)S(1)} %fusion.30), channel_id=1, replica_groups=mesh['src'=8,'dst'=32] {'src','dst'}, use_global_device_ids=true, to_apply=%region_17.18 | all-reduce | flops 40 | bytes 320 | tf_op jit(solution)/shard_map/psum | solution.py:104
  1322.2 108.4 %all-reduce.18.cloned.1.call-done = f32[8,8192]{1,0:T(8,128)} async-done(((f32[8,8192]{1,0:T(8,128)}), f32[8,8192]{1,0:T(8,128)}) %all-reduce.18.cloned.1.call-update) | async-done | bytes 262160 | tf_op jit(solution)/shard_map/psum | solution.py:77
  (200 shorter events, 46.3 us)
Async XLA Ops:
  7.2 403.5 %copy-start = (bf16[2048,128]{1,0:T(8,128)(2,1)S(1)}, bf16[2048,128]{1,0:T(8,128)(2,1)}, u32[]{:S(2)}) copy-start(bf16[2048,128]{1,0:T(8,128)(2,1)} %param.13) | copy-start | bytes 1572868
  8.7 324.0 %copy-start.7 = (s32[3,8]{1,0:T(4,128)S(1)}, s32[3,8]{1,0:T(4,128)}, u32[]{:S(2)}) copy-start(s32[3,8]{1,0:T(4,128)} %param.17) | copy-start | bytes 292
  8.7 324.1 %copy-start.8 = (bf16[1024,128]{1,0:T(8,128)(2,1)S(1)}, bf16[1024,128]{1,0:T(8,128)(2,1)}, u32[]{:S(2)}) copy-start(bf16[1024,128]{1,0:T(8,128)(2,1)} %param.14) | copy-start | bytes 786436
  8.7 388.0 %copy-start.1 = (f32[8,8192]{1,0:T(8,128)S(1)}, f32[8,8192]{1,0:T(8,128)}, u32[]{:S(2)}) copy-start(f32[8,8192]{1,0:T(8,128)} %param.18) | copy-start | bytes 786436
  85.3 325.3 %copy-start.6 = (f32[2048]{0:T(1024)S(1)}, f32[2048]{0:T(1024)}, u32[]{:S(2)}) copy-start(f32[2048]{0:T(1024)} %param.15) | copy-start | bytes 24580
  85.4 325.8 %copy-start.5 = (f32[8,2048]{1,0:T(8,128)S(1)}, f32[8,2048]{1,0:T(8,128)}, u32[]{:S(2)}) copy-start(f32[8,2048]{1,0:T(8,128)} %param.19) | copy-start | bytes 196612
  410.7 0.7 copy-start.4
  411.3 79.3 %all-reduce.8.cloned.1.call-start = ((), (), s32[]{:S(2)}) async-start(), calls=%async_computation | async-start | bytes 131072 | tf_op jit(solution)/shard_map/psum | solution.py:68
  412.0 126.1 %all-gather.5.cloned.1.call-start = ((), (), s32[]{:S(2)}) async-start(), calls=%async_computation.1 | async-start | bytes 2162688 | tf_op jit(solution)/shard_map/all_gather | solution.py:72
  553.0 74.8 %copy-start.2 = (f32[4,512,8,1]{1,2,0,3:T(8,128)}, f32[4,512,8,1]{1,2,0,3:T(8,128)S(1)}, u32[]{:S(2)}) copy-start(f32[4,512,8,1]{1,2,0,3:T(8,128)S(1)} %fusion.25) | copy-start | bytes 196612
  553.1 141.2 %all-reduce.10.cloned.1.call-start = ((), (), s32[]{:S(2)}) async-start(), calls=%async_computation.2 | async-start | bytes 131072 | tf_op jit(solution)/shard_map/psum | solution.py:68
  627.8 120.0 %all-gather.7.cloned.1.call-start = ((), (), s32[]{:S(2)}) async-start(), calls=%async_computation.3 | async-start | bytes 2162688 | tf_op jit(solution)/shard_map/all_gather | solution.py:72
  695.9 251.9 %all-reduce.14.cloned.1.call-start = ((), (), s32[]{:S(2)}) async-start(), calls=%async_computation.5 | async-start | bytes 524288 | tf_op jit(solution)/shard_map/psum | solution.py:77
  837.3 151.1 %all-gather.9.cloned.1.call-start = ((), (), s32[]{:S(2)}) async-start(), calls=%async_computation.6 | async-start | bytes 2359296 | tf_op jit(solution)/shard_map/all_gather | solution.py:80
  949.6 238.5 %all-reduce.16.cloned.1.call-start = ((), (), s32[]{:S(2)}) async-start(), calls=%async_computation.7 | async-start | bytes 524288 | tf_op jit(solution)/shard_map/psum | solution.py:77
  1078.3 150.3 %all-gather.11.cloned.1.call-start = ((), (), s32[]{:S(2)}) async-start(), calls=%async_computation.8 | async-start | bytes 2359296 | tf_op jit(solution)/shard_map/all_gather | solution.py:80
  1203.9 25.8 %copy-start.3 = (f32[4,512,8,1]{1,2,0,3:T(8,128)}, f32[4,512,8,1]{1,2,0,3:T(8,128)S(1)}, u32[]{:S(2)}) copy-start(f32[4,512,8,1]{1,2,0,3:T(8,128)S(1)} %fusion.23) | copy-start | bytes 196612
  1229.6 91.0 %all-reduce.12.cloned.1.call-start = ((), (), s32[]{:S(2)}) async-start(), calls=%async_computation.4 | async-start | bytes 131072 | tf_op jit(solution)/shard_map/psum | solution.py:68
  1230.4 200.2 %all-reduce.18.cloned.1.call-start = ((), (), s32[]{:S(2)}) async-start(), calls=%async_computation.9 | async-start | bytes 524288 | tf_op jit(solution)/shard_map/psum | solution.py:77
Sparse Core Ops, SparseCore 0:
  415.0 69.0 all-reduce.7
  492.3 45.7 all-gather.4
  627.9 66.3 all-reduce.9
  697.3 50.4 all-gather.6
  837.4 110.3 all-reduce.13
  950.2 38.1 all-gather.8
  1078.5 109.6 all-reduce.15
  1190.5 38.1 all-gather.10
  1233.3 69.0 all-reduce.11
  1320.7 109.8 all-reduce.17
where the time goes:
time: 1440 us
  blocking collectives  689 us (48%)
  waiting for transfers between devices  558 us (39%)
  matrix products  114 us (8%)
  other arithmetic  58.2 us (4%)
  between operations  14.4 us (1%)
    psum x3, waiting for transfers between devices, backward_finish(): beta_rows = lax.psum(partial_value, 'dst') / scale[:, None]  329 us
    psum x3, blocking collectives, local(): forward_total = lax.psum(forward_scale, ('src', 'dst'))  229 us
    psum x2, blocking collectives, local(): backward_total = lax.psum(backward_scale, ('src', 'dst'))  150 us
    psum x1, blocking collectives, local(): whole_mass = lax.psum(row_mass * jnp.exp(row_best - whole_best), 'dst')  124 us
    pmax x1, blocking collectives, local(): whole_best = lax.pmax(row_best, 'dst')  123 us
    all_gather x2, waiting for transfers between devices, forward_finish(): gathered = lax.all_gather(alpha_cols, 'dst', axis=1, tiled=True)  97.8 us
    psum x3, waiting for transfers between devices, forward_finish(): predicted = lax.psum(partial_value, 'src')  66.4 us
    psum x1, blocking collectives, local(): word_rows = lax.psum(looked.astype(jnp.bfloat16), 'dst')  63.7 us
  transfers between devices with their start and end apart: 10, of which 8 were waited for; matrix products, arithmetic and copies ran while one was open for 2% of the time, Pallas kernels for 0%

commit v1 on v0

v1 whole, which is shorter than its diff:
```python
import functools

import jax
import jax.numpy as jnp
from jax import lax
from jax.experimental import pallas as pl
from jax.experimental.pallas import tpu as pltpu
from jax.sharding import PartitionSpec as P

BLK = 512
CH = 256
STEPS = 3
TRACES = 8
TB = STEPS * TRACES
UNROLL = 4
very_negative = -1e30
VMEM_LIMIT = 52 * 1024 * 1024
NT = (((1,), (1,)), ((), ()))
NN = (((1,), (0,)), ((), ()))
f32 = jnp.float32
bf16 = jnp.bfloat16

OUT_AT = CH
WORD_AT = 2 * CH
BETA_AT = WORD_AT + 32
MISC_AT = BETA_AT + 48
BLOCK_ROWS = MISC_AT + 16


def tiles(x):
    return jnp.concatenate([x[:, :128], x[:, 128:]], axis=0)


def untile(x):
    return jnp.concatenate([x[:8], x[8:16]], axis=1)


def lanes(shape=(8, 128)):
    return lax.broadcasted_iota(jnp.int32, shape, len(shape) - 1)


def put_lanes(pairs):
    lane = lanes()
    out = jnp.zeros((8, 128), f32)
    for at, value in pairs:
        out = jnp.where(lane == at, value, out)
    return out


def inverse(x):
    return jnp.where(x > 0, 1.0 / jnp.where(x > 0, x, 1.0), 0.0)


def split3(x):
    hi = x.astype(bf16).astype(f32)
    rest = x - hi
    mid = rest.astype(bf16).astype(f32)
    return hi, mid, rest - mid


def place_of(p, A, H):
    return (p % A) * H + p // A


def pack_kernel(A, H, tok, words, dst, out, norm, beta, mask, block):
    vocab = words.shape[0]
    place = lax.axis_index("dst")
    ids = tok[...] - place * vocab
    onehot = jnp.where(lanes((TB, vocab)) == ids, 1.0, 0.0).astype(bf16)
    looked = lax.dot_general(onehot, words[...], NN, preferred_element_type=f32)
    looked = jnp.concatenate([looked, jnp.zeros((8, 128), f32)], axis=0).astype(bf16)
    RB = mask.shape[0]
    diag = lax.broadcasted_iota(jnp.int32, (RB, 128), 0) == lanes((RB, 128))
    for l in range(A):
        block[l, 0:CH] = dst[l * CH : (l + 1) * CH]
        block[l, OUT_AT : OUT_AT + CH] = out[l * CH : (l + 1) * CH]
        block[l, WORD_AT : WORD_AT + 32] = looked
        parts = split3(tiles(beta[:, l * CH : (l + 1) * CH]))
        block[l, BETA_AT : BETA_AT + 48] = jnp.concatenate(parts, axis=0).astype(bf16)
        column = mask[:, l // 2 : l // 2 + 1].astype(f32)
        mask_row = jnp.sum(jnp.where(diag, column, 0.0), axis=0, keepdims=True)
        norms = split3(norm[2 * l : 2 * l + 2])
        block[l, MISC_AT : MISC_AT + 16] = jnp.concatenate(
            [*norms, mask_row, jnp.zeros((9, 128), f32)], axis=0
        ).astype(bf16)


def table_kernel(
    A, H, recv, src, table, tops, best, pay, units, count,
    slots, mass, mask_v, mask_s, word_v, sems, mask_sem,
):
    RB = src.shape[0] // BLK
    for k in range(A):
        misc = recv[k, MISC_AT : MISC_AT + 16].astype(f32)
        mask_v[k : k + 1] = misc[6:7].astype(jnp.int32)
    copy = pltpu.make_async_copy(mask_v, mask_s, mask_sem)
    copy.start()
    best[...] = jnp.full(best.shape, very_negative, f32)
    mass[...] = jnp.zeros(mass.shape, f32)
    total = recv[0, WORD_AT : WORD_AT + 32].astype(f32)
    for k in range(1, A):
        total = total + recv[k, WORD_AT : WORD_AT + 32].astype(f32)
    word_v[...] = total
    copy.wait()

    def listing(i, c):
        for k in range(A):
            units[c] = i * A + k
            c = c + mask_s[k, i]
        return c

    cnt = lax.fori_loop(0, RB, listing, 0)
    count[0] = cnt

    def one(n, carry):
        u = units[n]
        i = u // A
        k = u - i * A
        cols = recv[k, 0:CH]
        for half in range(2):
            rows = src[pl.ds(i * BLK + half * CH, CH)]
            scores = lax.dot_general(cols, rows, NT, preferred_element_type=f32)
            top = jnp.max(scores, axis=0, keepdims=True)
            e = jnp.exp(scores - top)
            s = jnp.sum(e, axis=0, keepdims=True)
            at = slice(half * CH, (half + 1) * CH)
            slots[n, :, at] = e.astype(bf16)
            tops[i, pl.ds(k, 1), at] = top
            old = best[pl.ds(i, 1), at]
            new = jnp.maximum(old, top)
            mass[pl.ds(i, 1), at] = mass[pl.ds(i, 1), at] * jnp.exp(old - new) + s * jnp.exp(top - new)
            best[pl.ds(i, 1), at] = new
        pltpu.make_async_copy(slots.at[n], table.at[n], sems.at[n]).start()
        return carry

    lax.fori_loop(0, cnt, one, 0)
    per = TB // A
    mine = lax.axis_index("dst") // H
    words = word_v[pl.ds(mine * per, per)]
    for p in range(2 * RB):
        d = place_of(p, A, H)
        at = (p % 2) * CH
        i = p // 2
        pay[d, 0:1] = best[i : i + 1, at : at + 128]
        pay[d, 1:2] = best[i : i + 1, at + 128 : at + 256]
        pay[d, 2:3] = mass[i : i + 1, at : at + 128]
        pay[d, 3:4] = mass[i : i + 1, at + 128 : at + 256]
        pay[d, 4 : 4 + per] = words
        if pay.shape[1] > 4 + per:
            pay[d, 4 + per :] = jnp.zeros((pay.shape[1] - 4 - per, 128), f32)

    def drain(n, carry):
        pltpu.make_async_copy(slots.at[n], table.at[n], sems.at[n]).wait()
        return carry

    lax.fori_loop(0, cnt, drain, 0)


def start_table(table, slots, sems, cnt):
    def go(n, carry):
        pltpu.make_async_copy(table.at[n], slots.at[n], sems.at[n]).start()
        return carry

    lax.fori_loop(0, cnt, go, 0)


def sweep(A, table, slots, sems, units, cnt, unit_work):
    def some(it, carry):
        base = it * UNROLL
        for q in range(UNROLL):
            @pl.when(base + q < cnt)
            def _():
                n = base + q
                pltpu.make_async_copy(table.at[n], slots.at[n], sems.at[n]).wait()

        results = []
        for q in range(UNROLL):
            n = jnp.minimum(base + q, cnt - 1)
            u = units[n]
            i = u // A
            k = u - i * A
            results.append((i, k, base + q < cnt, unit_work(slots[n], i, k)))
        for i, k, valid, (adds) in results:
            for ref, index, value in adds:
                ref[index] += jnp.where(valid, value, 0.0)
        return carry

    lax.fori_loop(0, (cnt + UNROLL - 1) // UNROLL, some, 0)


def backward_unit(weights, factor, acc):
    def work(t, i, k):
        spread = lax.dot_general(weights[k], t, NN, preferred_element_type=f32)
        return [(acc, i, spread * factor(i, k))]

    return work


def scatter_rows(pay, acc, A, H, at=0):
    for p in range(2 * acc.shape[0]):
        part = acc[p // 2, :, (p % 2) * CH : (p % 2 + 1) * CH]
        pay[place_of(p, A, H), at : at + 16] = tiles(part)


def first_back_kernel(
    A, H, got, recv, tops, best, units, count, table,
    pay, share, emx, em_last, w_last, slots, acc, word_v, sems,
):
    cnt = count[0]
    start_table(table, slots, sems, cnt)
    D = A * H
    per = TB // A
    for l in range(A):
        total = got[l * H, 4 : 4 + per]
        for h in range(1, H):
            total = total + got[l * H + h, 4 : 4 + per]
        word_v[l * per : (l + 1) * per] = total
    words = word_v[0:TB].astype(bf16)
    top = got[0, 0:2]
    for d in range(1, D):
        top = jnp.maximum(top, got[d, 0:2])
    mass = jnp.zeros_like(top)
    for d in range(D):
        mass = mass + got[d, 2:4] * jnp.exp(got[d, 0:2] - top)
    log_total = top + jnp.log(mass)
    for d in range(D):
        share[d] = jnp.exp(got[d, 0:2] - log_total)
    mine = lax.axis_index("src")
    for k in range(A):
        logits = lax.dot_general(
            words, recv[k, OUT_AT : OUT_AT + CH], NT, preferred_element_type=f32
        )
        misc = recv[k, MISC_AT : MISC_AT + 16].astype(f32)
        norm = misc[0:2] + misc[2:4] + misc[4:6]
        norm = jnp.concatenate([norm[0:1], norm[1:2]], axis=1)
        em = jnp.exp(logits - norm)
        parts = recv[k, BETA_AT : BETA_AT + 48].astype(f32)
        beta = untile(parts[0:16] + parts[16:32] + parts[32:48])
        em_last[k] = em[16:24]
        w_last[k] = (em[16:24] * beta).astype(bf16)

        @pl.when(mine == k)
        def _():
            emx[...] = em

    acc[...] = jnp.zeros(acc.shape, f32)

    def factor(i, k):
        return jnp.exp(tops[i, pl.ds(k, 1)] - best[pl.ds(i, 1)])

    sweep(A, table, slots, sems, units, cnt, backward_unit(w_last, factor, acc))
    scatter_rows(pay, acc, A, H)
    tail = jnp.concatenate([log_total, jnp.zeros((6, 128), f32)], axis=0)
    for d in range(D):
        pay[d, 16:24] = tail


def send_weights(pay, carried, emission, A):
    whole = jnp.sum(carried[0:8] + carried[8:16], axis=1, keepdims=True)
    scaled = tiles(emission * (untile(carried) * inverse(whole)))
    for k in range(A):
        pay[k, 16:32] = scaled
    return whole


def first_forward_kernel(
    A, H, got, share, alpha, tops, emx, units, count, table,
    pay, factor, slots, acc, sems,
):
    cnt = count[0]
    start_table(table, slots, sems, cnt)
    D = A * H
    RB = tops.shape[0]
    for i in range(RB):
        d0 = place_of(2 * i, A, H)
        d1 = place_of(2 * i + 1, A, H)
        log_total = jnp.concatenate(
            [got[d0, 16:17], got[d0, 17:18], got[d1, 16:17], got[d1, 17:18]], axis=1
        )
        factor[i] = jnp.exp(tops[i] - log_total)
    acc[...] = jnp.zeros(acc.shape, f32)

    def work(t, i, k):
        mix = alpha[:, pl.ds(pl.multiple_of(i * BLK, BLK), BLK)] * factor[i, pl.ds(k, 1)]
        pred = lax.dot_general(mix.astype(bf16), t, NT, preferred_element_type=f32)
        return [(acc, k, pred)]

    sweep(A, table, slots, sems, units, cnt, work)
    for k in range(A):
        pay[k, 0:16] = tiles(acc[k])
    first = jnp.zeros((8, 128), f32)
    second = jnp.zeros((8, 128), f32)
    for d in range(D):
        first = first + got[d, 0:8] * share[d, 0:1]
        second = second + got[d, 8:16] * share[d, 1:2]
    whole = send_weights(pay, jnp.concatenate([first, second], axis=0), emx[8:16], A)
    for k in range(A):
        pay[k, 32:40] = put_lanes([(0, whole)])


def forward_kernel(
    A, H, t_at, last, got, factor, w_other, em, held, units, count, table, *rest
):
    if last:
        em_last, terms_in, pay, terms, carried_out, scales, slots, acc, alpha, sems = rest
    else:
        pay, terms, scales, slots, acc, alpha, sems = rest
    cnt = count[0]
    start_table(table, slots, sems, cnt)
    D = A * H
    RB = factor.shape[0]
    total = got[0, 16:24] + got[0, 24:32]
    for d in range(1, D):
        total = total + (got[d, 16:24] + got[d, 24:32])
    rows_sum = jnp.sum(total, axis=1, keepdims=True)
    scale = inverse(rows_sum)
    for p in range(2 * RB):
        u = got[place_of(p, A, H), 16:32]
        alpha[p // 2, :, (p % 2) * CH : (p % 2 + 1) * CH] = untile(u) * scale
    acc[...] = jnp.zeros(acc.shape, f32)
    terms[...] = terms_in[...] if last else jnp.zeros(terms.shape, f32)
    lane = lanes()

    def work(t, i, k):
        mix = alpha[i] * factor[i, pl.ds(k, 1)]
        pred = lax.dot_general(mix.astype(bf16), t, NT, preferred_element_type=f32)
        term = jnp.sum(pred * w_other[k].astype(f32), axis=1, keepdims=True)
        return [(acc, k, pred), (terms, k, jnp.where(lane == t_at * RB + i, term, 0.0))]

    sweep(A, table, slots, sems, units, cnt, work)
    for k in range(A):
        pay[k, 0:16] = tiles(acc[k])
    cols_sum = got[0, 32:40]
    for d in range(1, D):
        cols_sum = cols_sum + got[d, 32:40]
    norm = inverse(cols_sum)
    first = jnp.zeros((8, 128), f32)
    second = jnp.zeros((8, 128), f32)
    for d in range(D):
        weight = got[d, 32:40] * norm
        first = first + got[d, 0:8] * weight
        second = second + got[d, 8:16] * weight
    carried = jnp.concatenate([first, second], axis=0)
    sigma = (held[...] * norm)[:, 0:1]
    if not last:
        whole = send_weights(pay, carried, em[0:8], A)
        for k in range(A):
            pay[k, 32:40] = put_lanes([(0, whole), (1, rows_sum)])
        scales[...] = put_lanes([(0, sigma), (1, rows_sum)])
        return
    carried_out[...] = carried
    reach = jnp.zeros((8, 128), f32)
    every = jnp.zeros((8, 128), f32)
    for k in range(A):
        product = acc[k] * em_last[k]
        reach = reach + (product[:, :128] + product[:, 128:])
        every = every + terms[k]
    reach = jnp.sum(reach, axis=1, keepdims=True)
    whole = jnp.sum(first + second, axis=1, keepdims=True)
    ratio_one = em[:, 0:1]
    pairs = []
    for t in range(STEPS):
        here = (lane >= t * RB) & (lane < (t + 1) * RB)
        pairs.append(jnp.sum(jnp.where(here, every, 0.0), axis=1, keepdims=True))
    tail = put_lanes(
        [(0, rows_sum), (1, reach), (2, whole), (3, pairs[0] * sigma), (4, pairs[1] * ratio_one), (5, pairs[2])]
    )
    for k in range(A):
        pay[k, 16:24] = tail
    scales[...] = put_lanes([(0, sigma), (1, ratio_one), (2, rows_sum)])


def back_kernel(
    A, H, states, t_at, got, factor, emx, units, count, table, *rest
):
    if t_at is None:
        pay, weights, held, slots, acc, sems = rest
    else:
        alpha, terms_in, scales_in, pay, terms, ratio, held, slots, acc, weights, sems = rest
    cnt = count[0]
    start_table(table, slots, sems, cnt)
    D = A * H
    RB = factor.shape[0]
    cols_sum = got[0, 32:40, 0:1]
    for k in range(1, A):
        cols_sum = cols_sum + got[k, 32:40, 0:1]
    norm = inverse(cols_sum)
    for k in range(A):
        weights[k] = (untile(got[k, 16:32]) * (got[k, 32:40, 0:1] * norm)).astype(bf16)
    acc[...] = jnp.zeros(acc.shape, f32)
    if t_at is None:
        work = backward_unit(weights, lambda i, k: factor[i, pl.ds(k, 1)], acc)
    else:
        terms[...] = terms_in[...]
        lane = lanes()

        def work(t, i, k):
            spread = lax.dot_general(weights[k], t, NN, preferred_element_type=f32)
            fac = factor[i, pl.ds(k, 1)]
            mix = (alpha[:, pl.ds(pl.multiple_of(i * BLK, BLK), BLK)] * fac).astype(bf16)
            term = jnp.sum(mix.astype(f32) * spread, axis=1, keepdims=True)
            return [
                (acc, i, spread * fac),
                (terms, k, jnp.where(lane == t_at * RB + i, term, 0.0)),
            ]

    sweep(A, table, slots, sems, units, cnt, work)
    scatter_rows(pay, acc, A, H)
    if t_at is None:
        pred = got[0, 0:16]
        for s in range(1, A):
            pred = pred + got[s, 0:16]
        emission = emx[0:8]
    else:
        rows_sum = got[0, 32:40, 1:2]
        for s in range(1, A):
            rows_sum = rows_sum + got[s, 32:40, 1:2]
        inv = inverse(rows_sum)
        pred = jnp.zeros((16, 128), f32)
        for s in range(A):
            weight = got[s, 32:40, 1:2] * inv * states
            pred = pred + got[s, 0:16] * jnp.concatenate([weight, weight], axis=0)
        emission = emx[8:16]
        rho = scales_in[:, 1:2] * inv
        ratio[...] = put_lanes([(0, rho * scales_in[:, 0:1])])
    product = tiles(untile(pred) * emission)
    wide = jnp.broadcast_to(cols_sum, (8, 128))
    held[...] = wide
    for d in range(D):
        pay[d, 16:32] = product
        pay[d, 32:40] = wide


def gather_kernel(A, H, states, RB, got, carried, emx, terms, scales, pay):
    rows_sum = got[0, 16:24, 0:1]
    for s in range(1, A):
        rows_sum = rows_sum + got[s, 16:24, 0:1]
    inv = inverse(rows_sum)
    pred = jnp.zeros((16, 128), f32)
    tail = jnp.zeros((8, 128), f32)
    lane = lanes()
    for s in range(A):
        share = got[s, 16:24, 0:1] * inv
        weight = share * states
        pred = pred + got[s, 0:16] * jnp.concatenate([weight, weight], axis=0)
        piece = got[s, 16:24]
        piece = jnp.where(lane == 1, piece * weight, piece)
        piece = jnp.where(lane == 5, piece * share, piece)
        tail = tail + piece
    product = tiles(untile(pred) * emx[16:24])
    tail = jnp.where(lane < 6, tail, 0.0)
    tail = jnp.concatenate([tail[:, 64:], tail[:, :64]], axis=1)
    sigma = scales[:, 0:1]
    one = scales[:, 1:2]
    rho = scales[:, 2:3] * inv
    mult = jnp.where(lane < RB, sigma, jnp.where(lane < 2 * RB, one, jnp.where(lane < 3 * RB, rho, 0.0)))
    for k in range(A):
        last = jnp.where(lane < 3 * RB, terms[k] * mult, 0.0) + tail
        for h in range(H):
            pay[k * H + h, 32:40] = last
    back = carried[...]
    for d in range(A * H):
        pay[d, 0:16] = back
        pay[d, 16:32] = product


def finish_kernel(A, H, states, scale, RB, got, alpha, beta, counts):
    D = A * H
    lane = lanes()
    total = got[0, 32:40]
    for d in range(1, D):
        total = total + got[d, 32:40]
    total = jnp.where(lane >= 64, total, 0.0)
    reach = total[:, 65:66]
    whole = total[:, 66:67]
    for_beta = states / whole
    for_alpha = states / reach
    inv = jnp.zeros((8, 128), f32)
    for t in range(STEPS):
        here = (lane >= t * RB) & (lane < (t + 1) * RB)
        inv = jnp.where(here, scale / total[:, 67 + t : 68 + t], inv)
    for p in range(2 * RB):
        beta[:, p * CH : (p + 1) * CH] = untile(got[place_of(p, A, H), 0:16]) * for_beta
    mine = lax.rem(lax.axis_index("dst"), H)
    row = lax.broadcasted_iota(jnp.int32, (RB, 128), 0)
    wide = lanes((RB, 128))
    picks = (wide == row) | (wide == row + RB) | (wide == row + 2 * RB)
    out = jnp.zeros((RB, 128), f32)
    for l in range(A):
        alpha[:, l * CH : (l + 1) * CH] = untile(got[l * H + mine, 16:32]) * for_alpha
        line = jnp.where(lane < 3 * RB, got[l * H + mine, 32:40] * inv, 0.0)
        line = jnp.sum(line, axis=0, keepdims=True)
        column = jnp.sum(jnp.where(picks, line, 0.0), axis=1, keepdims=True)
        out = out + jnp.where(wide == l // 2, column, 0.0)
    counts[...] = out[:, : counts.shape[1]]


def call(body, outs, scratch=(), big=False):
    vm = pl.BlockSpec(memory_space=pltpu.VMEM)
    sm = pl.BlockSpec(memory_space=pltpu.SMEM)
    hbm = pl.BlockSpec(memory_space=pl.ANY)
    kinds = {"v": vm, "s": sm, "h": hbm}

    def run(kinds_in, *args):
        return pl.pallas_call(
            body,
            in_specs=[kinds[c] for c in kinds_in],
            out_specs=[kinds[c] for c, _, _ in outs],
            out_shape=[jax.ShapeDtypeStruct(s, d) for _, s, d in outs],
            scratch_shapes=list(scratch),
            compiler_params=pltpu.CompilerParams(
                vmem_limit_bytes=VMEM_LIMIT if big else 16 * 1024 * 1024
            ),
        )(*args)

    return run


def local(
    src_emb, dst_emb, out_emb, word_table, log_norm, block_mask, tokens, alpha_start, beta_end
):
    A = lax.axis_size("src")
    D = lax.axis_size("dst")
    H = D // A
    rows = src_emb.shape[0]
    RB = rows // BLK
    states = float(rows * A)
    NB = RB * A
    UN = RB * A
    VM = pltpu.VMEM
    groups = [[h + H * k for k in range(A)] for h in range(H)]
    over_dst = lambda x: lax.all_to_all(x, "dst", 0, 0)
    over_src = lambda x: lax.all_to_all(x, "src", 0, 0)
    part = functools.partial

    (block,) = call(part(pack_kernel, A, H), [("v", (A, BLOCK_ROWS, 128), bf16)], big=True)(
        "vvvvvvv", tokens.reshape(TB, 1), word_table, dst_emb, out_emb,
        log_norm.reshape(-1, 128), beta_end, block_mask,
    )
    recv = lax.all_to_all(block, "dst", 0, 0, axis_index_groups=groups)

    per = TB // A
    pay_rows = -(-(4 + per) // 8) * 8
    slots = VM((UN, CH, BLK), bf16)
    sems = pltpu.SemaphoreType.DMA((UN,))
    acc_rows = VM((RB, 8, BLK), f32)
    acc_cols = VM((A, 8, CH), f32)
    table, tops, best, pay, units, count = call(
        part(table_kernel, A, H),
        [
            ("h", (UN, CH, BLK), bf16),
            ("v", (RB, A, BLK), f32),
            ("v", (RB, BLK), f32),
            ("v", (D, pay_rows, 128), f32),
            ("s", (UN,), jnp.int32),
            ("s", (1,), jnp.int32),
        ],
        [
            slots, VM((RB, BLK), f32), VM((A, 128), jnp.int32),
            pltpu.SMEM((A, 128), jnp.int32), VM((32, 128), f32), sems, pltpu.SemaphoreType.DMA(()),
        ],
        big=True,
    )("vv", recv, src_emb)
    got = over_dst(pay)

    pay, share, emx, em_last, w_last = call(
        part(first_back_kernel, A, H),
        [
            ("v", (D, 24, 128), f32),
            ("v", (D, 2, 128), f32),
            ("v", (TB, CH), f32),
            ("v", (A, 8, CH), f32),
            ("v", (A, 8, CH), bf16),
        ],
        [slots, acc_rows, VM((TB, 128), f32), sems],
        big=True,
    )("vvvvssh", got, recv, tops, best, units, count, table)
    got = over_dst(pay)

    pay, factor = call(
        part(first_forward_kernel, A, H),
        [("v", (A, 40, 128), f32), ("v", (RB, A, BLK), f32)],
        [slots, acc_cols, sems],
        big=True,
    )("vvvvvssh", got, share, alpha_start, tops, emx, units, count, table)
    got = over_src(pay)

    pay, w_two, held = call(
        part(back_kernel, A, H, states, None),
        [("v", (D, 40, 128), f32), ("v", (A, 8, CH), bf16), ("v", (8, 128), f32)],
        [slots, acc_rows, sems],
        big=True,
    )("vvvssh", got, factor, emx, units, count, table)
    got = over_dst(pay)

    pay, terms, scales = call(
        part(forward_kernel, A, H, 1, False),
        [("v", (A, 40, 128), f32), ("v", (A, 8, 128), f32), ("v", (8, 128), f32)],
        [slots, acc_cols, acc_rows, sems],
        big=True,
    )("vvvvvssh", got, factor, w_two, emx, held, units, count, table)
    got = over_src(pay)

    pay, terms, ratio, held = call(
        part(back_kernel, A, H, states, 0),
        [
            ("v", (D, 40, 128), f32), ("v", (A, 8, 128), f32),
            ("v", (8, 128), f32), ("v", (8, 128), f32),
        ],
        [slots, acc_rows, VM((A, 8, CH), bf16), sems],
        big=True,
    )("vvvsshvvv", got, factor, emx, units, count, table, alpha_start, terms, scales)
    got = over_dst(pay)

    pay, terms, carried, scales = call(
        part(forward_kernel, A, H, 2, True),
        [
            ("v", (A, 24, 128), f32), ("v", (A, 8, 128), f32),
            ("v", (16, 128), f32), ("v", (8, 128), f32),
        ],
        [slots, acc_cols, acc_rows, sems],
        big=True,
    )("vvvvvsshvv", got, factor, w_last, ratio, held, units, count, table, em_last, terms)
    got = over_src(pay)

    (pay,) = call(part(gather_kernel, A, H, states, RB), [("v", (D, 40, 128), f32)])(
        "vvvvv", got, carried, emx, terms, scales
    )
    got = over_dst(pay)

    alpha_end, beta_start, counts = call(
        part(finish_kernel, A, H, states, NB * NB / TB, RB),
        [
            ("v", (8, A * CH), f32),
            ("v", (8, rows), f32),
            ("v", (RB, block_mask.shape[1]), f32),
        ],
    )("v", got)
    swaps = [
        (a * D + b * H + h, b * D + a * H + h) for a in range(A) for b in range(A) for h in range(H)
    ]
    alpha_end = lax.ppermute(alpha_end, ("src", "dst"), swaps)
    return (alpha_end, beta_start, counts)


def solution(mesh):
    return jax.shard_map(
        local,
        mesh=mesh,
        in_specs=(
            P("src", None),
            P("dst", None),
            P("dst", None),
            P("dst", None),
            P("dst"),
            P("src", "dst"),
            P(),
            P(None, "src"),
            P(None, "dst"),
        ),
        out_specs=(P(None, "dst"), P(None, "src"), P("src", "dst")),
        check_vma=False,
    )
```

time: 1440 us -> 219 us (0.15)
  waiting for transfers between devices: 558 us -> 10.9 us
  blocking collectives: 689 us -> 151 us
  matrix products: 114 us -> 0 us
  other arithmetic: 58.2 us -> 0 us
  Pallas kernels: 0 us -> 44.3 us
    psum x7 -> x0, blocking collectives: 566 us -> none  [the longest x3 229 us: local(): forward_total = lax.psum(forward_scale, ('src', 'dst'))]
    psum x6 -> x0, waiting for transfers between devices: 395 us -> none  [the longest x3 329 us: backward_finish(): beta_rows = lax.psum(partial_value, 'dst') / scale[:, None]]
    all_gather x4 -> x0, waiting for transfers between devices: 161 us -> none  [the longest x2 97.8 us: forward_finish(): gathered = lax.all_gather(alpha_cols, 'dst', axis=1, tiled=True)]
    all_to_all x0 -> x9, blocking collectives: none -> 151 us  [the longest x5 86.1 us: local(): over_dst = lambda x: lax.all_to_all(x, 'dst', 0, 0)]
    pmax x1 -> x0, blocking collectives: 123 us -> none  [local(): whole_best = lax.pmax(row_best, 'dst')]
    dot_general x24 -> x0, matrix products: 114 us -> none  [the longest x3 41.8 us: local(): jnp.einsum('bijr,irjc->bjc', mix_terms, transit, preferred_element_type=j...]
    pallas_call x0 -> x10, Pallas kernels: none -> 44.3 us  [run(): pl.pallas_call(body, in_specs=[kinds[c] for c in kinds_in], out_specs=[ki...]
    dynamic_update_slice x16 -> x0, other arithmetic: 32.5 us -> none  [local(): lax.scan(table_block, 0, (src_emb.reshape(row_blocks, BLK, emb_width), bl...]
  transfers between devices with their start and end apart: 10 -> 1, of which waited for: 8 -> 1; matrix products, arithmetic and copies ran while one was open for 2% -> 0% of each run, Pallas kernels for 0% -> 0%
where the time goes in v1:
time: 219 us; the launch traced here: 218 us
  blocking collectives  151 us (69%)
  Pallas kernels  44.3 us (20%)
  waiting for transfers between devices  10.9 us (5%)
  local copies, waits for them, and re-layouts  7.38 us (3%)
  starting transfers between devices  4.08 us (2%)
    all_to_all x5, blocking collectives, local(): over_dst = lambda x: lax.all_to_all(x, 'dst', 0, 0)  86.1 us
    pallas_call x10, Pallas kernels, run(): pl.pallas_call(body, in_specs=[kinds[c] for c in kinds_in], out_specs=[ki...  44.3 us
    all_to_all x3, blocking collectives, local(): over_src = lambda x: lax.all_to_all(x, 'src', 0, 0)  43.5 us
    all_to_all x1, blocking collectives, local(): recv = lax.all_to_all(block, 'dst', 0, 0, axis_index_groups=groups)  21.2 us
    ppermute x1, waiting for transfers between devices, local(): alpha_end = lax.ppermute(alpha_end, ('src', 'dst'), swaps)  10.9 us
    unnamed x17, local copies, waits for them, and re-layouts  6.62 us
  transfers between devices with their start and end apart: 1, of which 1 were waited for; matrix products, arithmetic and copies ran while one was open for 0% of the time, Pallas kernels for 0%

profile of v1, /device:TPU:31, one launch (start us, length us, event | category | flops | bytes accessed | tf_op | source)
XLA Modules:
  0.0 218.3 jit_solution(14427553027325220836)
XLA Ops:
  0.6 0.8 copy.13.mask
  1.4 0.8 reshape.14.tok
  2.1 0.0 copy-start.2
  2.1 1.0 copy-done.2
  3.2 0.0 copy-start.3
  3.2 1.0 copy-done.3
  4.2 0.0 copy-start.4
  4.2 0.9 copy-done.4
  5.2 0.0 copy-start.5
  5.2 0.8 copy-done.5
  6.0 0.0 copy-start.6
  6.0 0.7 copy-done.6
  6.7 1.3 shard_map.112
  8.0 21.2 %all_to_all.45.recv = bf16[8,608,128]{2,1,0:T(8,128)(2,1)S(1)} all-to-all(bf16[8,608,128]{2,1,0:T(8,128)(2,1)} %shard_map.112), channel_id=1, replica_groups={{0,4,8,12,16,20,24,28},{1,5,9,13,17,21,25,29},{2,6,10,14,18,22,26,30},{..., dimensions={0} | all-to-all | bytes 2490368 | tf_op jit(solution)/shard_map/all_to_all | solution.py:540
  29.3 0.0 copy-start
  29.3 10.1 %shard_map.113 = (bf16[128,256,512]{2,1,0:T(8,128)(2,1)}, f32[16,8,512]{2,1,0:T(8,128)S(1)}, f32[16,512]{1,0:T(8,128)S(1)}, f32[32,8,128]{2,1,0:T(8,128)S(1)}, s32[128]{0:T(128)S(1)}, /*index=5*/s32[1]{0:T(128)}) custom-call(bf16[8,608,128]{2,1,0:T(8,128)(2,1)S(1)} %all_to_all.45.recv, bf16[8192,128]{1,0:T(8,128)(2,1)} %src.1), custom_call_target="tpu_custom_call" | custom-call | tf_op jit(solution)/shard_map/pallas_call | solution.py:505
  39.3 16.5 %all_to_all.46.got = f32[32,8,128]{2,1,0:T(8,128)S(1)} all-to-all(f32[32,8,128]{2,1,0:T(8,128)S(1)} %get-tuple-element.33), channel_id=1, replica_groups=mesh['src'=8,'dst'=32] {'dst'}, dimensions={0} | all-to-all | bytes 262144 | tf_op jit(solution)/shard_map/all_to_all | solution.py:532
  55.9 0.0 copy-done
  55.9 0.0 copy-start.1
  55.9 5.6 %shard_map.114 = (f32[32,24,128]{2,1,0:T(8,128)S(1)}, f32[32,2,128]{2,1,0:T(2,128)S(1)}, f32[24,256]{1,0:T(8,128)S(1)}, f32[8,8,256]{2,1,0:T(8,128)S(1)}, bf16[8,8,256]{2,1,0:T(8,128)(2,1)S(1)}) custom-call(f32[32,8,128]{2,1,0:T(8,128)S(1)} %all_to_all.46.got, bf16[8,608,128]{2,1,0:T(8,128)(2,1)} %copy-done, f32[16,8,512]{2,1,0:T(8,128)S(1)} %get-tuple-element.34.tops, ...), custom_call_target="tpu_custom_call" | custom-call | tf_op jit(solution)/shard_map/pallas_call | solution.py:505
  61.5 14.4 %all_to_all.47.got = f32[32,24,128]{2,1,0:T(8,128)S(1)} all-to-all(f32[32,24,128]{2,1,0:T(8,128)S(1)} %get-tuple-element.39), channel_id=1, replica_groups=mesh['src'=8,'dst'=32] {'dst'}, dimensions={0} | all-to-all | bytes 786432 | tf_op jit(solution)/shard_map/all_to_all | solution.py:532
  75.9 0.0 copy-done.1
  75.9 5.3 %shard_map.115 = (f32[8,40,128]{2,1,0:T(8,128)S(1)}, f32[16,8,512]{2,1,0:T(8,128)S(1)}) custom-call(f32[32,24,128]{2,1,0:T(8,128)S(1)} %all_to_all.47.got, f32[32,2,128]{2,1,0:T(2,128)S(1)} %get-tuple-element.40.share, f32[8,8192]{1,0:T(8,128)S(1)} %copy-done.1, f32[16,8,512]{2,1,0:T(8,128)S(1)} %get-tuple-element.34.tops, ...), custom_call_target="tpu_custom_call" | custom-call | tf_op jit(solution)/shard_map/pallas_call | solution.py:505
  81.2 20.9 %all_to_all.48.got = f32[8,40,128]{2,1,0:T(8,128)S(1)} all-to-all(f32[8,40,128]{2,1,0:T(8,128)S(1)} %get-tuple-element.42), channel_id=1, replica_groups=mesh['src'=8,'dst'=32] {'src'}, dimensions={0} | all-to-all | bytes 327680 | tf_op jit(solution)/shard_map/all_to_all | solution.py:533
  102.1 4.7 %shard_map.116 = (f32[32,40,128]{2,1,0:T(8,128)S(1)}, bf16[8,8,256]{2,1,0:T(8,128)(2,1)S(1)}, f32[8,128]{1,0:T(8,128)S(1)}) custom-call(f32[8,40,128]{2,1,0:T(8,128)S(1)} %all_to_all.48.got, f32[16,8,512]{2,1,0:T(8,128)S(1)} %get-tuple-element.43.factor, f32[24,256]{1,0:T(8,128)S(1)} %get-tuple-element.41.emx.em, s32[128]{0:T(128)S(1)} %get-tuple-element.36.units, ...), custom_call_target="tpu_custom_call" | custom-call | tf_op jit(solution)/shard_map/pallas_call | solution.py:505
  106.9 18.0 %all_to_all.49.got = f32[32,40,128]{2,1,0:T(8,128)S(1)} all-to-all(f32[32,40,128]{2,1,0:T(8,128)S(1)} %get-tuple-element.44), channel_id=1, replica_groups=mesh['src'=8,'dst'=32] {'dst'}, dimensions={0} | all-to-all | bytes 1310720 | tf_op jit(solution)/shard_map/all_to_all | solution.py:532
  124.9 5.6 %shard_map.117 = (f32[8,40,128]{2,1,0:T(8,128)S(1)}, f32[8,8,128]{2,1,0:T(8,128)S(1)}, f32[8,128]{1,0:T(8,128)S(1)}) custom-call(f32[32,40,128]{2,1,0:T(8,128)S(1)} %all_to_all.49.got, f32[16,8,512]{2,1,0:T(8,128)S(1)} %get-tuple-element.43.factor, bf16[8,8,256]{2,1,0:T(8,128)(2,1)S(1)} %get-tuple-element.45.w_other, ...), custom_call_target="tpu_custom_call" | custom-call | tf_op jit(solution)/shard_map/pallas_call | solution.py:505
  130.5 11.7 %all_to_all.50.got = f32[8,40,128]{2,1,0:T(8,128)S(1)} all-to-all(f32[8,40,128]{2,1,0:T(8,128)S(1)} %get-tuple-element.47), channel_id=1, replica_groups=mesh['src'=8,'dst'=32] {'src'}, dimensions={0} | all-to-all | bytes 327680 | tf_op jit(solution)/shard_map/all_to_all | solution.py:533
  142.2 5.0 %shard_map.118 = (f32[32,40,128]{2,1,0:T(8,128)S(1)}, f32[8,8,128]{2,1,0:T(8,128)S(1)}, f32[8,128]{1,0:T(8,128)S(1)}, f32[8,128]{1,0:T(8,128)S(1)}) custom-call(f32[8,40,128]{2,1,0:T(8,128)S(1)} %all_to_all.50.got, f32[16,8,512]{2,1,0:T(8,128)S(1)} %get-tuple-element.43.factor, f32[24,256]{1,0:T(8,128)S(1)} %get-tuple-element.41.emx.em, ...), custom_call_target="tpu_custom_call" | custom-call | tf_op jit(solution)/shard_map/pallas_call | solution.py:505
  147.2 18.9 %all_to_all.51.got = f32[32,40,128]{2,1,0:T(8,128)S(1)} all-to-all(f32[32,40,128]{2,1,0:T(8,128)S(1)} %get-tuple-element.50), channel_id=1, replica_groups=mesh['src'=8,'dst'=32] {'dst'}, dimensions={0} | all-to-all | bytes 1310720 | tf_op jit(solution)/shard_map/all_to_all | solution.py:532
  166.1 5.6 %shard_map.119 = (f32[8,24,128]{2,1,0:T(8,128)S(1)}, f32[8,8,128]{2,1,0:T(8,128)S(1)}, f32[16,128]{1,0:T(8,128)S(1)}, f32[8,128]{1,0:T(8,128)S(1)}) custom-call(f32[32,40,128]{2,1,0:T(8,128)S(1)} %all_to_all.51.got, f32[16,8,512]{2,1,0:T(8,128)S(1)} %get-tuple-element.43.factor, bf16[8,8,256]{2,1,0:T(8,128)(2,1)S(1)} %get-tuple-element.51.w_other, ...), custom_call_target="tpu_custom_call" | custom-call | tf_op jit(solution)/shard_map/pallas_call | solution.py:505
  171.7 10.9 %all_to_all.52.got = f32[8,24,128]{2,1,0:T(8,128)S(1)} all-to-all(f32[8,24,128]{2,1,0:T(8,128)S(1)} %get-tuple-element.56), channel_id=1, replica_groups=mesh['src'=8,'dst'=32] {'src'}, dimensions={0} | all-to-all | bytes 196608 | tf_op jit(solution)/shard_map/all_to_all | solution.py:533
  182.6 0.2 shard_map.120
  182.8 18.3 %all_to_all.53.got = f32[32,40,128]{2,1,0:T(8,128)S(1)} all-to-all(f32[32,40,128]{2,1,0:T(8,128)S(1)} %shard_map.120), channel_id=1, replica_groups=mesh['src'=8,'dst'=32] {'dst'}, dimensions={0} | all-to-all | bytes 1310720 | tf_op jit(solution)/shard_map/all_to_all | solution.py:532
  201.0 0.9 shard_map.121
  202.0 4.1 %collective-permute-start = (f32[8,2048]{1,0:T(8,128)S(1)}, f32[8,2048]{1,0:T(8,128)S(1)}, u32[]{:S(2)}, u32[]{:S(2)}) collective-permute-start(f32[8,2048]{1,0:T(8,128)S(1)} %get-tuple-element.60), channel_id=1, source_target_pairs={{0,0},{1,1},{2,2},{3,3},{4,32},{5,33},{6,34},{7,35},{8,64},{9,65},... | collective-permute-start | bytes 196616 | tf_op jit(solution)/shard_map/ppermute | solution.py:642
  206.0 0.7 copy.14
  206.7 10.9 %collective-permute-done = f32[8,2048]{1,0:T(8,128)S(1)} collective-permute-done((f32[8,2048]{1,0:T(8,128)S(1)}, f32[8,2048]{1,0:T(8,128)S(1)}, u32[]{:S(2)}, u32[]{:S(2)}) %collective-permute-start) | collective-permute-done | bytes 65568 | tf_op jit(solution)/shard_map/ppermute | solution.py:642
  217.6 0.6 copy.16
Async XLA Ops:
  2.1 1.0 copy-start.2
  3.2 1.0 copy-start.3
  4.2 0.9 copy-start.4
  5.2 0.8 copy-start.5
  6.0 0.7 copy-start.6
  29.3 26.6 %copy-start = (bf16[8,608,128]{2,1,0:T(8,128)(2,1)}, bf16[8,608,128]{2,1,0:T(8,128)(2,1)S(1)}, u32[]{:S(2)}) copy-start(bf16[8,608,128]{2,1,0:T(8,128)(2,1)S(1)} %all_to_all.45.recv) | copy-start | bytes 3735556
  55.9 20.1 %copy-start.1 = (f32[8,8192]{1,0:T(8,128)S(1)}, f32[8,8192]{1,0:T(8,128)}, u32[]{:S(2)}) copy-start(f32[8,8192]{1,0:T(8,128)} %rest_0_.1) | copy-start | bytes 786436
  202.0 15.7 %collective-permute-start = (f32[8,2048]{1,0:T(8,128)S(1)}, f32[8,2048]{1,0:T(8,128)S(1)}, u32[]{:S(2)}, u32[]{:S(2)}) collective-permute-start(f32[8,2048]{1,0:T(8,128)S(1)} %get-tuple-element.60), channel_id=1, source_target_pairs={{0,0},{1,1},{2,2},{3,3},{4,32},{5,33},{6,34},{7,35},{8,64},{9,65},... | collective-permute-start | bytes 196616 | tf_op jit(solution)/shard_map/ppermute | solution.py:642

commit v2 on v1

--- a/solution.py
+++ b/solution.py
@@ -14,7 +14,7 @@
 TB = STEPS * TRACES
 UNROLL = 4
 very_negative = -1e30
-VMEM_LIMIT = 52 * 1024 * 1024
+VMEM_LIMIT = int(20.5 * 1024 * 1024)
 NT = (((1,), (1,)), ((), ()))
 NN = (((1,), (0,)), ((), ()))
 f32 = jnp.float32
@@ -87,7 +87,7 @@
 
 def table_kernel(
     A, H, recv, src, table, tops, best, pay, units, count,
-    slots, mass, mask_v, mask_s, word_v, sems, mask_sem,
+    mass, mask_v, mask_s, word_v, mask_sem,
 ):
     RB = src.shape[0] // BLK
     for k in range(A):
@@ -124,13 +124,12 @@
             e = jnp.exp(scores - top)
             s = jnp.sum(e, axis=0, keepdims=True)
             at = slice(half * CH, (half + 1) * CH)
-            slots[n, :, at] = e.astype(bf16)
+            table[n, :, at] = e.astype(bf16)
             tops[i, pl.ds(k, 1), at] = top
             old = best[pl.ds(i, 1), at]
             new = jnp.maximum(old, top)
             mass[pl.ds(i, 1), at] = mass[pl.ds(i, 1), at] * jnp.exp(old - new) + s * jnp.exp(top - new)
             best[pl.ds(i, 1), at] = new
-        pltpu.make_async_copy(slots.at[n], table.at[n], sems.at[n]).start()
         return carry
 
     lax.fori_loop(0, cnt, one, 0)
@@ -149,37 +148,17 @@
         if pay.shape[1] > 4 + per:
             pay[d, 4 + per :] = jnp.zeros((pay.shape[1] - 4 - per, 128), f32)
 
-    def drain(n, carry):
-        pltpu.make_async_copy(slots.at[n], table.at[n], sems.at[n]).wait()
-        return carry
-
-    lax.fori_loop(0, cnt, drain, 0)
-
-
-def start_table(table, slots, sems, cnt):
-    def go(n, carry):
-        pltpu.make_async_copy(table.at[n], slots.at[n], sems.at[n]).start()
-        return carry
-
-    lax.fori_loop(0, cnt, go, 0)
-
-
-def sweep(A, table, slots, sems, units, cnt, unit_work):
+
+def sweep(A, table, units, cnt, unit_work):
     def some(it, carry):
         base = it * UNROLL
-        for q in range(UNROLL):
-            @pl.when(base + q < cnt)
-            def _():
-                n = base + q
-                pltpu.make_async_copy(table.at[n], slots.at[n], sems.at[n]).wait()
-
         results = []
         for q in range(UNROLL):
             n = jnp.minimum(base + q, cnt - 1)
             u = units[n]
             i = u // A
             k = u - i * A
-            results.append((i, k, base + q < cnt, unit_work(slots[n], i, k)))
+            results.append((i, k, base + q < cnt, unit_work(table[n], i, k)))
         for i, k, valid, (adds) in results:
             for ref, index, value in adds:
                 ref[index] += jnp.where(valid, value, 0.0)
@@ -204,10 +183,9 @@
 
 def first_back_kernel(
     A, H, got, recv, tops, best, units, count, table,
-    pay, share, emx, em_last, w_last, slots, acc, word_v, sems,
+    pay, share, emx, em_last, w_last, acc, word_v,
 ):
     cnt = count[0]
-    start_table(table, slots, sems, cnt)
     D = A * H
     per = TB // A
     for l in range(A):
@@ -248,7 +226,7 @@
     def factor(i, k):
         return jnp.exp(tops[i, pl.ds(k, 1)] - best[pl.ds(i, 1)])
 
-    sweep(A, table, slots, sems, units, cnt, backward_unit(w_last, factor, acc))
+    sweep(A, table, units, cnt, backward_unit(w_last, factor, acc))
     scatter_rows(pay, acc, A, H)
     tail = jnp.concatenate([log_total, jnp.zeros((6, 128), f32)], axis=0)
     for d in range(D):
@@ -265,10 +243,9 @@
 
 def first_forward_kernel(
     A, H, got, share, alpha, tops, emx, units, count, table,
-    pay, factor, slots, acc, sems,
+    pay, factor, acc,
 ):
     cnt = count[0]
-    start_table(table, slots, sems, cnt)
     D = A * H
     RB = tops.shape[0]
     for i in range(RB):
@@ -285,7 +262,7 @@
         pred = lax.dot_general(mix.astype(bf16), t, NT, preferred_element_type=f32)
         return [(acc, k, pred)]
 
-    sweep(A, table, slots, sems, units, cnt, work)
+    sweep(A, table, units, cnt, work)
     for k in range(A):
         pay[k, 0:16] = tiles(acc[k])
     first = jnp.zeros((8, 128), f32)
@@ -302,11 +279,10 @@
     A, H, t_at, last, got, factor, w_other, em, held, units, count, table, *rest
 ):
     if last:
-        em_last, terms_in, pay, terms, carried_out, scales, slots, acc, alpha, sems = rest
+        em_last, terms_in, pay, terms, carried_out, scales, acc, alpha = rest
     else:
-        pay, terms, scales, slots, acc, alpha, sems = rest
+        pay, terms, scales, acc, alpha = rest
     cnt = count[0]
-    start_table(table, slots, sems, cnt)
     D = A * H
     RB = factor.shape[0]
     total = got[0, 16:24] + got[0, 24:32]
@@ -327,7 +303,7 @@
         term = jnp.sum(pred * w_other[k].astype(f32), axis=1, keepdims=True)
         return [(acc, k, pred), (terms, k, jnp.where(lane == t_at * RB + i, term, 0.0))]
 
-    sweep(A, table, slots, sems, units, cnt, work)
+    sweep(A, table, units, cnt, work)
     for k in range(A):
         pay[k, 0:16] = tiles(acc[k])
     cols_sum = got[0, 32:40]
@@ -374,11 +350,10 @@
     A, H, states, t_at, got, factor, emx, units, count, table, *rest
 ):
     if t_at is None:
-        pay, weights, held, slots, acc, sems = rest
+        pay, weights, held, acc = rest
     else:
-        alpha, terms_in, scales_in, pay, terms, ratio, held, slots, acc, weights, sems = rest
+        alpha, terms_in, scales_in, pay, terms, ratio, held, acc, weights = rest
     cnt = count[0]
-    start_table(table, slots, sems, cnt)
     D = A * H
     RB = factor.shape[0]
     cols_sum = got[0, 32:40, 0:1]
@@ -404,7 +379,7 @@
                 (terms, k, jnp.where(lane == t_at * RB + i, term, 0.0)),
             ]
 
-    sweep(A, table, slots, sems, units, cnt, work)
+    sweep(A, table, units, cnt, work)
     scatter_rows(pay, acc, A, H)
     if t_at is None:
         pred = got[0, 0:16]
@@ -499,19 +474,26 @@
     vm = pl.BlockSpec(memory_space=pltpu.VMEM)
     sm = pl.BlockSpec(memory_space=pltpu.SMEM)
     hbm = pl.BlockSpec(memory_space=pl.ANY)
-    kinds = {"v": vm, "s": sm, "h": hbm}
+    kinds = {"v": vm, "s": sm, "h": hbm, "m": vm}
 
     def run(kinds_in, *args):
         return pl.pallas_call(
             body,
             in_specs=[kinds[c] for c in kinds_in],
             out_specs=[kinds[c] for c, _, _ in outs],
-            out_shape=[jax.ShapeDtypeStruct(s, d) for _, s, d in outs],
+            out_shape=[
+                pltpu.VMEM(s, d) if c == "m" else jax.ShapeDtypeStruct(s, d) for c, s, d in outs
+            ],
             scratch_shapes=list(scratch),
             compiler_params=pltpu.CompilerParams(
                 vmem_limit_bytes=VMEM_LIMIT if big else 16 * 1024 * 1024
             ),
-        )(*args)
+        )(
+            *[
+                pltpu.with_memory_space_constraint(a, pltpu.VMEM) if c == "m" else a
+                for c, a in zip(kinds_in, args)
+            ]
+        )
 
     return run
 
@@ -541,14 +523,12 @@
 
     per = TB // A
     pay_rows = -(-(4 + per) // 8) * 8
-    slots = VM((UN, CH, BLK), bf16)
-    sems = pltpu.SemaphoreType.DMA((UN,))
     acc_rows = VM((RB, 8, BLK), f32)
     acc_cols = VM((A, 8, CH), f32)
     table, tops, best, pay, units, count = call(
         part(table_kernel, A, H),
         [
-            ("h", (UN, CH, BLK), bf16),
+            ("m", (UN, CH, BLK), bf16),
             ("v", (RB, A, BLK), f32),
             ("v", (RB, BLK), f32),
             ("v", (D, pay_rows, 128), f32),
@@ -556,8 +536,8 @@
             ("s", (1,), jnp.int32),
         ],
         [
-            slots, VM((RB, BLK), f32), VM((A, 128), jnp.int32),
-            pltpu.SMEM((A, 128), jnp.int32), VM((32, 128), f32), sems, pltpu.SemaphoreType.DMA(()),
+            VM((RB, BLK), f32), VM((A, 128), jnp.int32),
+            pltpu.SMEM((A, 128), jnp.int32), VM((32, 128), f32), pltpu.SemaphoreType.DMA(()),
         ],
         big=True,
     )("vv", recv, src_emb)
@@ -572,33 +552,33 @@
             ("v", (A, 8, CH), f32),
             ("v", (A, 8, CH), bf16),
         ],
-        [slots, acc_rows, VM((TB, 128), f32), sems],
+        [acc_rows, VM((TB, 128), f32)],
         big=True,
-    )("vvvvssh", got, recv, tops, best, units, count, table)
+    )("vvvvssm", got, recv, tops, best, units, count, table)
     got = over_dst(pay)
 
     pay, factor = call(
         part(first_forward_kernel, A, H),
         [("v", (A, 40, 128), f32), ("v", (RB, A, BLK), f32)],
-        [slots, acc_cols, sems],
+        [acc_cols],
         big=True,
-    )("vvvvvssh", got, share, alpha_start, tops, emx, units, count, table)
+    )("vvvvvssm", got, share, alpha_start, tops, emx, units, count, table)
     got = over_src(pay)
 
     pay, w_two, held = call(
         part(back_kernel, A, H, states, None),
         [("v", (D, 40, 128), f32), ("v", (A, 8, CH), bf16), ("v", (8, 128), f32)],
-        [slots, acc_rows, sems],
+        [acc_rows],
         big=True,
-    )("vvvssh", got, factor, emx, units, count, table)
+    )("vvvssm", got, factor, emx, units, count, table)
     got = over_dst(pay)
 
     pay, terms, scales = call(
         part(forward_kernel, A, H, 1, False),
         [("v", (A, 40, 128), f32), ("v", (A, 8, 128), f32), ("v", (8, 128), f32)],
-        [slots, acc_cols, acc_rows, sems],
+        [acc_cols, acc_rows],
         big=True,
-    )("vvvvvssh", got, factor, w_two, emx, held, units, count, table)
+    )("vvvvvssm", got, factor, w_two, emx, held, units, count, table)
     got = over_src(pay)
 
     pay, terms, ratio, held = call(
@@ -607,9 +587,9 @@
             ("v", (D, 40, 128), f32), ("v", (A, 8, 128), f32),
             ("v", (8, 128), f32), ("v", (8, 128), f32),
         ],
-        [slots, acc_rows, VM((A, 8, CH), bf16), sems],
+        [acc_rows, VM((A, 8, CH), bf16)],
         big=True,
-    )("vvvsshvvv", got, factor, emx, units, count, table, alpha_start, terms, scales)
+    )("vvvssmvvv", got, factor, emx, units, count, table, alpha_start, terms, scales)
     got = over_dst(pay)
 
     pay, terms, carried, scales = call(
@@ -618,9 +598,9 @@
             ("v", (A, 24, 128), f32), ("v", (A, 8, 128), f32),
             ("v", (16, 128), f32), ("v", (8, 128), f32),
         ],
-        [slots, acc_cols, acc_rows, sems],
+        [acc_cols, acc_rows],
         big=True,
-    )("vvvvvsshvv", got, factor, w_last, ratio, held, units, count, table, em_last, terms)
+    )("vvvvvssmvv", got, factor, w_last, ratio, held, units, count, table, em_last, terms)
     got = over_src(pay)
 
     (pay,) = call(part(gather_kernel, A, H, states, RB), [("v", (D, 40, 128), f32)])(

time: 219 us -> 204 us (0.932)
  Pallas kernels: 44.3 us -> 32.7 us
  blocking collectives: 151 us -> 147 us
    pallas_call x10, Pallas kernels: 44.3 us -> 32.7 us  [run(): pl.pallas_call(body, in_specs=[kinds[c] for c in kinds_in], out_specs=[ki...]
    all_to_all x5, blocking collectives: 86.1 us -> 81.2 us  [local(): over_dst = lambda x: lax.all_to_all(x, 'dst', 0, 0)]
    unnamed x17 -> x15, local copies, waits for them, and re-layouts: 6.62 us -> 6.62 us
where the time goes in v2:
time: 204 us; the launch traced here: 203 us
  blocking collectives  147 us (72%)
  Pallas kernels  32.7 us (16%)
  waiting for transfers between devices  10.5 us (5%)
  local copies, waits for them, and re-layouts  7.37 us (4%)
  starting transfers between devices  4.54 us (2%)
    all_to_all x5, blocking collectives, local(): over_dst = lambda x: lax.all_to_all(x, 'dst', 0, 0)  81.2 us
    all_to_all x3, blocking collectives, local(): over_src = lambda x: lax.all_to_all(x, 'src', 0, 0)  44.5 us
    pallas_call x10, Pallas kernels, run(): pl.pallas_call(body, in_specs=[kinds[c] for c in kinds_in], out_specs=[ki...  32.7 us
    all_to_all x1, blocking collectives, local(): recv = lax.all_to_all(block, 'dst', 0, 0, axis_index_groups=groups)  21.2 us
    ppermute x1, waiting for transfers between devices, local(): alpha_end = lax.ppermute(alpha_end, ('src', 'dst'), swaps)  10.5 us
    unnamed x15, local copies, waits for them, and re-layouts  6.62 us
    ppermute x1, starting transfers between devices, local(): alpha_end = lax.ppermute(alpha_end, ('src', 'dst'), swaps)  4.54 us
  transfers between devices with their start and end apart: 1, of which 1 were waited for; matrix products, arithmetic and copies ran while one was open for 0% of the time, Pallas kernels for 0%

profile of v2, /device:TPU:31, one launch (start us, length us, event | category | flops | bytes accessed | tf_op | source)
XLA Modules:
  0.0 202.7 jit_solution(8572546996968991413)
XLA Ops:
  0.6 0.8 copy.13.mask
  1.4 0.8 reshape.14.tok
  2.1 0.0 copy-start.1
  2.1 1.0 copy-done.1
  3.2 0.0 copy-start.2
  3.2 1.0 copy-done.2
  4.2 0.0 copy-start.3
  4.2 0.9 copy-done.3
  5.2 0.0 copy-start.4
  5.2 0.8 copy-done.4
  6.0 0.0 copy-start.5
  6.0 0.7 copy-done.5
  6.7 0.2 shard_map.112
  7.0 21.2 %all_to_all.45.recv = bf16[8,608,128]{2,1,0:T(8,128)(2,1)} all-to-all(bf16[8,608,128]{2,1,0:T(8,128)(2,1)S(1)} %shard_map.112), channel_id=1, replica_groups={{0,4,8,12,16,20,24,28},{1,5,9,13,17,21,25,29},{2,6,10,14,18,22,26,30},{..., dimensions={0} | all-to-all | bytes 2490368 | tf_op jit(solution)/shard_map/all_to_all | solution.py:522
  28.1 10.0 %shard_map.113 = (bf16[128,256,512]{2,1,0:T(8,128)(2,1)S(1)}, f32[16,8,512]{2,1,0:T(8,128)S(1)}, f32[16,512]{1,0:T(8,128)S(1)}, f32[32,8,128]{2,1,0:T(8,128)S(1)}, s32[128]{0:T(128)S(1)}, /*index=5*/s32[1]{0:T(128)}) custom-call(bf16[8,608,128]{2,1,0:T(8,128)(2,1)} %all_to_all.45.recv, bf16[8192,128]{1,0:T(8,128)(2,1)} %src.1), custom_call_target="tpu_custom_call" | custom-call | tf_op jit(solution)/shard_map/pallas_call | solution.py:480
  38.1 13.7 %all_to_all.46.got = f32[32,8,128]{2,1,0:T(8,128)S(1)} all-to-all(f32[32,8,128]{2,1,0:T(8,128)S(1)} %get-tuple-element.33), channel_id=1, replica_groups=mesh['src'=8,'dst'=32] {'dst'}, dimensions={0} | all-to-all | bytes 262144 | tf_op jit(solution)/shard_map/all_to_all | solution.py:514
  51.8 0.0 copy-start
  51.8 4.6 %shard_map.114 = (f32[32,24,128]{2,1,0:T(8,128)S(1)}, f32[32,2,128]{2,1,0:T(2,128)S(1)}, f32[24,256]{1,0:T(8,128)S(1)}, f32[8,8,256]{2,1,0:T(8,128)S(1)}, bf16[8,8,256]{2,1,0:T(8,128)(2,1)S(1)}) custom-call(f32[32,8,128]{2,1,0:T(8,128)S(1)} %all_to_all.46.got, bf16[8,608,128]{2,1,0:T(8,128)(2,1)} %all_to_all.45.recv, ...), custom_call_target="tpu_custom_call" | custom-call | tf_op jit(solution)/shard_map/pallas_call | solution.py:480
  56.4 14.0 %all_to_all.47.got = f32[32,24,128]{2,1,0:T(8,128)S(1)} all-to-all(f32[32,24,128]{2,1,0:T(8,128)S(1)} %get-tuple-element.39), channel_id=1, replica_groups=mesh['src'=8,'dst'=32] {'dst'}, dimensions={0} | all-to-all | bytes 786432 | tf_op jit(solution)/shard_map/all_to_all | solution.py:514
  70.4 0.0 copy-done
  70.4 3.3 %shard_map.115 = (f32[8,40,128]{2,1,0:T(8,128)S(1)}, f32[16,8,512]{2,1,0:T(8,128)S(1)}) custom-call(f32[32,24,128]{2,1,0:T(8,128)S(1)} %all_to_all.47.got, f32[32,2,128]{2,1,0:T(2,128)S(1)} %get-tuple-element.40.share, f32[8,8192]{1,0:T(8,128)S(1)} %copy-done, f32[16,8,512]{2,1,0:T(8,128)S(1)} %get-tuple-element.34.tops, ...), custom_call_target="tpu_custom_call" | custom-call | tf_op jit(solution)/shard_map/pallas_call | solution.py:480
  73.7 23.0 %all_to_all.48.got = f32[8,40,128]{2,1,0:T(8,128)S(1)} all-to-all(f32[8,40,128]{2,1,0:T(8,128)S(1)} %get-tuple-element.42), channel_id=1, replica_groups=mesh['src'=8,'dst'=32] {'src'}, dimensions={0} | all-to-all | bytes 327680 | tf_op jit(solution)/shard_map/all_to_all | solution.py:515
  96.7 2.6 %shard_map.116 = (f32[32,40,128]{2,1,0:T(8,128)S(1)}, bf16[8,8,256]{2,1,0:T(8,128)(2,1)S(1)}, f32[8,128]{1,0:T(8,128)S(1)}) custom-call(f32[8,40,128]{2,1,0:T(8,128)S(1)} %all_to_all.48.got, f32[16,8,512]{2,1,0:T(8,128)S(1)} %get-tuple-element.43.factor, f32[24,256]{1,0:T(8,128)S(1)} %get-tuple-element.41.emx.em, s32[128]{0:T(128)S(1)} %get-tuple-element.36.units, ...), custom_call_target="tpu_custom_call" | custom-call | tf_op jit(solution)/shard_map/pallas_call | solution.py:480
  99.4 16.6 %all_to_all.49.got = f32[32,40,128]{2,1,0:T(8,128)S(1)} all-to-all(f32[32,40,128]{2,1,0:T(8,128)S(1)} %get-tuple-element.44), channel_id=1, replica_groups=mesh['src'=8,'dst'=32] {'dst'}, dimensions={0} | all-to-all | bytes 1310720 | tf_op jit(solution)/shard_map/all_to_all | solution.py:514
  116.0 3.8 %shard_map.117 = (f32[8,40,128]{2,1,0:T(8,128)S(1)}, f32[8,8,128]{2,1,0:T(8,128)S(1)}, f32[8,128]{1,0:T(8,128)S(1)}) custom-call(f32[32,40,128]{2,1,0:T(8,128)S(1)} %all_to_all.49.got, f32[16,8,512]{2,1,0:T(8,128)S(1)} %get-tuple-element.43.factor, bf16[8,8,256]{2,1,0:T(8,128)(2,1)S(1)} %get-tuple-element.45.w_other, ...), custom_call_target="tpu_custom_call" | custom-call | tf_op jit(solution)/shard_map/pallas_call | solution.py:480
  119.8 11.1 %all_to_all.50.got = f32[8,40,128]{2,1,0:T(8,128)S(1)} all-to-all(f32[8,40,128]{2,1,0:T(8,128)S(1)} %get-tuple-element.47), channel_id=1, replica_groups=mesh['src'=8,'dst'=32] {'src'}, dimensions={0} | all-to-all | bytes 327680 | tf_op jit(solution)/shard_map/all_to_all | solution.py:515
  130.9 3.1 %shard_map.118 = (f32[32,40,128]{2,1,0:T(8,128)S(1)}, f32[8,8,128]{2,1,0:T(8,128)S(1)}, f32[8,128]{1,0:T(8,128)S(1)}, f32[8,128]{1,0:T(8,128)S(1)}) custom-call(f32[8,40,128]{2,1,0:T(8,128)S(1)} %all_to_all.50.got, f32[16,8,512]{2,1,0:T(8,128)S(1)} %get-tuple-element.43.factor, f32[24,256]{1,0:T(8,128)S(1)} %get-tuple-element.41.emx.em, ...), custom_call_target="tpu_custom_call" | custom-call | tf_op jit(solution)/shard_map/pallas_call | solution.py:480
  134.0 18.5 %all_to_all.51.got = f32[32,40,128]{2,1,0:T(8,128)S(1)} all-to-all(f32[32,40,128]{2,1,0:T(8,128)S(1)} %get-tuple-element.50), channel_id=1, replica_groups=mesh['src'=8,'dst'=32] {'dst'}, dimensions={0} | all-to-all | bytes 1310720 | tf_op jit(solution)/shard_map/all_to_all | solution.py:514
  152.5 3.9 %shard_map.119 = (f32[8,24,128]{2,1,0:T(8,128)S(1)}, f32[8,8,128]{2,1,0:T(8,128)S(1)}, f32[16,128]{1,0:T(8,128)S(1)}, f32[8,128]{1,0:T(8,128)S(1)}) custom-call(f32[32,40,128]{2,1,0:T(8,128)S(1)} %all_to_all.51.got, f32[16,8,512]{2,1,0:T(8,128)S(1)} %get-tuple-element.43.factor, bf16[8,8,256]{2,1,0:T(8,128)(2,1)S(1)} %get-tuple-element.51.w_other, ...), custom_call_target="tpu_custom_call" | custom-call | tf_op jit(solution)/shard_map/pallas_call | solution.py:480
  156.4 10.4 %all_to_all.52.got = f32[8,24,128]{2,1,0:T(8,128)S(1)} all-to-all(f32[8,24,128]{2,1,0:T(8,128)S(1)} %get-tuple-element.56), channel_id=1, replica_groups=mesh['src'=8,'dst'=32] {'src'}, dimensions={0} | all-to-all | bytes 196608 | tf_op jit(solution)/shard_map/all_to_all | solution.py:515
  166.8 0.2 shard_map.120
  167.0 18.5 %all_to_all.53.got = f32[32,40,128]{2,1,0:T(8,128)S(1)} all-to-all(f32[32,40,128]{2,1,0:T(8,128)S(1)} %shard_map.120), channel_id=1, replica_groups=mesh['src'=8,'dst'=32] {'dst'}, dimensions={0} | all-to-all | bytes 1310720 | tf_op jit(solution)/shard_map/all_to_all | solution.py:514
  185.4 0.9 shard_map.121
  186.4 4.5 %collective-permute-start = (f32[8,2048]{1,0:T(8,128)S(1)}, f32[8,2048]{1,0:T(8,128)S(1)}, u32[]{:S(2)}, u32[]{:S(2)}) collective-permute-start(f32[8,2048]{1,0:T(8,128)S(1)} %get-tuple-element.60), channel_id=1, source_target_pairs={{0,0},{1,1},{2,2},{3,3},{4,32},{5,33},{6,34},{7,35},{8,64},{9,65},... | collective-permute-start | bytes 196616 | tf_op jit(solution)/shard_map/ppermute | solution.py:622
  190.9 0.7 copy.14
  191.6 10.5 %collective-permute-done = f32[8,2048]{1,0:T(8,128)S(1)} collective-permute-done((f32[8,2048]{1,0:T(8,128)S(1)}, f32[8,2048]{1,0:T(8,128)S(1)}, u32[]{:S(2)}, u32[]{:S(2)}) %collective-permute-start) | collective-permute-done | bytes 65568 | tf_op jit(solution)/shard_map/ppermute | solution.py:622
  202.0 0.6 copy.16
Async XLA Ops:
  2.1 1.0 copy-start.1
  3.2 1.0 copy-start.2
  4.2 0.9 copy-start.3
  5.2 0.8 copy-start.4
  6.0 0.7 copy-start.5
  51.8 18.6 %copy-start = (f32[8,8192]{1,0:T(8,128)S(1)}, f32[8,8192]{1,0:T(8,128)}, u32[]{:S(2)}) copy-start(f32[8,8192]{1,0:T(8,128)} %rest_0_.1) | copy-start | bytes 786436
  186.4 15.7 %collective-permute-start = (f32[8,2048]{1,0:T(8,128)S(1)}, f32[8,2048]{1,0:T(8,128)S(1)}, u32[]{:S(2)}, u32[]{:S(2)}) collective-permute-start(f32[8,2048]{1,0:T(8,128)S(1)} %get-tuple-element.60), channel_id=1, source_target_pairs={{0,0},{1,1},{2,2},{3,3},{4,32},{5,33},{6,34},{7,35},{8,64},{9,65},... | collective-permute-start | bytes 196616 | tf_op jit(solution)/shard_map/ppermute | solution.py:622

commit v3 on v2

--- a/solution.py
+++ b/solution.py
@@ -12,7 +12,8 @@
 STEPS = 3
 TRACES = 8
 TB = STEPS * TRACES
-UNROLL = 4
+UNROLL = 8
+TABLE_UNROLL = 4
 very_negative = -1e30
 VMEM_LIMIT = int(20.5 * 1024 * 1024)
 NT = (((1,), (1,)), ((), ()))
@@ -62,32 +63,56 @@
     return (p % A) * H + p // A
 
 
-def pack_kernel(A, H, tok, words, dst, out, norm, beta, mask, block):
+def pack_kernel(
+    A, H, tok, words, dst, out, norm, beta, mask,
+    block, words_v, norm_v, beta_v, mask_v, tok_s, sems,
+):
+    copies = [
+        pltpu.make_async_copy(words, words_v, sems.at[0]),
+        pltpu.make_async_copy(norm, norm_v, sems.at[1]),
+        pltpu.make_async_copy(beta, beta_v, sems.at[2]),
+        pltpu.make_async_copy(mask, mask_v, sems.at[3]),
+    ]
+    for l in range(A):
+        rows = slice(l * CH, (l + 1) * CH)
+        copies.append(pltpu.make_async_copy(dst.at[rows], block.at[l, 0:CH], sems.at[4 + 2 * l]))
+        copies.append(
+            pltpu.make_async_copy(out.at[rows], block.at[l, OUT_AT : OUT_AT + CH], sems.at[5 + 2 * l])
+        )
+    tok_copy = pltpu.make_async_copy(tok, tok_s, sems.at[4 + 2 * A])
+    tok_copy.start()
+    for copy in copies:
+        copy.start()
+    tok_copy.wait()
     vocab = words.shape[0]
     place = lax.axis_index("dst")
-    ids = tok[...] - place * vocab
-    onehot = jnp.where(lanes((TB, vocab)) == ids, 1.0, 0.0).astype(bf16)
-    looked = lax.dot_general(onehot, words[...], NN, preferred_element_type=f32)
+    row = lax.broadcasted_iota(jnp.int32, (TB, 1), 0)
+    ids = jnp.zeros((TB, 1), jnp.int32)
+    for r in range(TB):
+        ids = jnp.where(row == r, tok_s[r // TRACES, r % TRACES], ids)
+    onehot = jnp.where(lanes((TB, vocab)) == ids - place * vocab, 1.0, 0.0).astype(bf16)
+    for copy in copies[:4]:
+        copy.wait()
+    looked = lax.dot_general(onehot, words_v[...], NN, preferred_element_type=f32)
     looked = jnp.concatenate([looked, jnp.zeros((8, 128), f32)], axis=0).astype(bf16)
-    RB = mask.shape[0]
-    diag = lax.broadcasted_iota(jnp.int32, (RB, 128), 0) == lanes((RB, 128))
+    width, RB = mask_v.shape
     for l in range(A):
-        block[l, 0:CH] = dst[l * CH : (l + 1) * CH]
-        block[l, OUT_AT : OUT_AT + CH] = out[l * CH : (l + 1) * CH]
         block[l, WORD_AT : WORD_AT + 32] = looked
-        parts = split3(tiles(beta[:, l * CH : (l + 1) * CH]))
+        parts = split3(tiles(beta_v[:, l * CH : (l + 1) * CH]))
         block[l, BETA_AT : BETA_AT + 48] = jnp.concatenate(parts, axis=0).astype(bf16)
-        column = mask[:, l // 2 : l // 2 + 1].astype(f32)
-        mask_row = jnp.sum(jnp.where(diag, column, 0.0), axis=0, keepdims=True)
-        norms = split3(norm[2 * l : 2 * l + 2])
+        mask_row = mask_v[l // 2 : l // 2 + 1].astype(f32)
+        mask_row = jnp.concatenate([mask_row, jnp.zeros((1, 128 - RB), f32)], axis=1)
+        norms = split3(norm_v[2 * l : 2 * l + 2])
         block[l, MISC_AT : MISC_AT + 16] = jnp.concatenate(
             [*norms, mask_row, jnp.zeros((9, 128), f32)], axis=0
         ).astype(bf16)
+    for copy in copies[4:]:
+        copy.wait()
 
 
 def table_kernel(
     A, H, recv, src, table, tops, best, pay, units, count,
-    mass, mask_v, mask_s, word_v, mask_sem,
+    sums, mass, mask_v, mask_s, word_v, mask_sem,
 ):
     RB = src.shape[0] // BLK
     for k in range(A):
@@ -95,8 +120,8 @@
         mask_v[k : k + 1] = misc[6:7].astype(jnp.int32)
     copy = pltpu.make_async_copy(mask_v, mask_s, mask_sem)
     copy.start()
-    best[...] = jnp.full(best.shape, very_negative, f32)
-    mass[...] = jnp.zeros(mass.shape, f32)
+    tops[...] = jnp.full(tops.shape, very_negative, f32)
+    sums[...] = jnp.zeros(sums.shape, f32)
     total = recv[0, WORD_AT : WORD_AT + 32].astype(f32)
     for k in range(1, A):
         total = total + recv[k, WORD_AT : WORD_AT + 32].astype(f32)
@@ -112,27 +137,31 @@
     cnt = lax.fori_loop(0, RB, listing, 0)
     count[0] = cnt
 
-    def one(n, carry):
-        u = units[n]
-        i = u // A
-        k = u - i * A
-        cols = recv[k, 0:CH]
-        for half in range(2):
-            rows = src[pl.ds(i * BLK + half * CH, CH)]
-            scores = lax.dot_general(cols, rows, NT, preferred_element_type=f32)
-            top = jnp.max(scores, axis=0, keepdims=True)
-            e = jnp.exp(scores - top)
-            s = jnp.sum(e, axis=0, keepdims=True)
-            at = slice(half * CH, (half + 1) * CH)
-            table[n, :, at] = e.astype(bf16)
-            tops[i, pl.ds(k, 1), at] = top
-            old = best[pl.ds(i, 1), at]
-            new = jnp.maximum(old, top)
-            mass[pl.ds(i, 1), at] = mass[pl.ds(i, 1), at] * jnp.exp(old - new) + s * jnp.exp(top - new)
-            best[pl.ds(i, 1), at] = new
+    def some(it, carry):
+        for q in range(TABLE_UNROLL):
+            n = jnp.minimum(it * TABLE_UNROLL + q, cnt - 1)
+            u = units[n]
+            i = u // A
+            k = u - i * A
+            cols = recv[k, 0:CH]
+            unit_tops, unit_sums = [], []
+            for part in range(BLK // 128):
+                rows = src[pl.ds(pl.multiple_of(i * BLK + part * 128, 128), 128)]
+                scores = lax.dot_general(cols, rows, NT, preferred_element_type=f32)
+                top = jnp.max(scores, axis=0, keepdims=True)
+                e = jnp.exp(scores - top)
+                unit_tops.append(top)
+                unit_sums.append(jnp.sum(e, axis=0, keepdims=True))
+                table[n, :, part * 128 : (part + 1) * 128] = e.astype(bf16)
+            tops[i, pl.ds(k, 1)] = jnp.concatenate(unit_tops, axis=1)
+            sums[i, pl.ds(k, 1)] = jnp.concatenate(unit_sums, axis=1)
         return carry
 
-    lax.fori_loop(0, cnt, one, 0)
+    lax.fori_loop(0, (cnt + TABLE_UNROLL - 1) // TABLE_UNROLL, some, 0)
+    for i in range(RB):
+        row_best = jnp.max(tops[i], axis=0, keepdims=True)
+        best[i : i + 1] = row_best
+        mass[i : i + 1] = jnp.sum(sums[i] * jnp.exp(tops[i] - row_best), axis=0, keepdims=True)
     per = TB // A
     mine = lax.axis_index("dst") // H
     words = word_v[pl.ds(mine * per, per)]
@@ -175,10 +204,21 @@
     return work
 
 
-def scatter_rows(pay, acc, A, H, at=0):
+def halves(x):
+    hi = x.astype(bf16)
+    return hi, (x - hi.astype(f32)).astype(bf16)
+
+
+def scatter_rows(pay, acc, A, H, exact=False):
     for p in range(2 * acc.shape[0]):
-        part = acc[p // 2, :, (p % 2) * CH : (p % 2 + 1) * CH]
-        pay[place_of(p, A, H), at : at + 16] = tiles(part)
+        part = tiles(acc[p // 2, :, (p % 2) * CH : (p % 2 + 1) * CH])
+        d = place_of(p, A, H)
+        if exact:
+            hi, lo = halves(part)
+            pay[d, 0:16] = hi
+            pay[d, 16:32] = lo
+        else:
+            pay[d, 0:16] = part.astype(bf16)
 
 
 def first_back_kernel(
@@ -228,9 +268,9 @@
 
     sweep(A, table, units, cnt, backward_unit(w_last, factor, acc))
     scatter_rows(pay, acc, A, H)
-    tail = jnp.concatenate([log_total, jnp.zeros((6, 128), f32)], axis=0)
+    tail = jnp.concatenate([*split3(log_total), jnp.zeros((10, 128), f32)], axis=0).astype(bf16)
     for d in range(D):
-        pay[d, 16:24] = tail
+        pay[d, 16:32] = tail
 
 
 def send_weights(pay, carried, emission, A):
@@ -249,11 +289,12 @@
     D = A * H
     RB = tops.shape[0]
     for i in range(RB):
-        d0 = place_of(2 * i, A, H)
-        d1 = place_of(2 * i + 1, A, H)
-        log_total = jnp.concatenate(
-            [got[d0, 16:17], got[d0, 17:18], got[d1, 16:17], got[d1, 17:18]], axis=1
-        )
+        pieces = []
+        for p in (2 * i, 2 * i + 1):
+            total = got[place_of(p, A, H), 16:32].astype(f32)
+            total = total[0:2] + total[2:4] + total[4:6]
+            pieces += [total[0:1], total[1:2]]
+        log_total = jnp.concatenate(pieces, axis=1)
         factor[i] = jnp.exp(tops[i] - log_total)
     acc[...] = jnp.zeros(acc.shape, f32)
 
@@ -268,8 +309,9 @@
     first = jnp.zeros((8, 128), f32)
     second = jnp.zeros((8, 128), f32)
     for d in range(D):
-        first = first + got[d, 0:8] * share[d, 0:1]
-        second = second + got[d, 8:16] * share[d, 1:2]
+        piece = got[d, 0:16].astype(f32)
+        first = first + piece[0:8] * share[d, 0:1]
+        second = second + piece[8:16] * share[d, 1:2]
     whole = send_weights(pay, jnp.concatenate([first, second], axis=0), emx[8:16], A)
     for k in range(A):
         pay[k, 32:40] = put_lanes([(0, whole)])
@@ -285,13 +327,15 @@
     cnt = count[0]
     D = A * H
     RB = factor.shape[0]
-    total = got[0, 16:24] + got[0, 24:32]
+    at = 32 if last else 16
+    total = got[0, at : at + 16].astype(f32)
     for d in range(1, D):
-        total = total + (got[d, 16:24] + got[d, 24:32])
+        total = total + got[d, at : at + 16].astype(f32)
+    total = total[0:8] + total[8:16]
     rows_sum = jnp.sum(total, axis=1, keepdims=True)
     scale = inverse(rows_sum)
     for p in range(2 * RB):
-        u = got[place_of(p, A, H), 16:32]
+        u = got[place_of(p, A, H), at : at + 16].astype(f32)
         alpha[p // 2, :, (p % 2) * CH : (p % 2 + 1) * CH] = untile(u) * scale
     acc[...] = jnp.zeros(acc.shape, f32)
     terms[...] = terms_in[...] if last else jnp.zeros(terms.shape, f32)
@@ -306,16 +350,21 @@
     sweep(A, table, units, cnt, work)
     for k in range(A):
         pay[k, 0:16] = tiles(acc[k])
-    cols_sum = got[0, 32:40]
+    spans = [got[d, at + 16 : at + 32].astype(f32) for d in range(D)]
+    spans = [x[0:8] + x[8:16] for x in spans]
+    cols_sum = spans[0]
     for d in range(1, D):
-        cols_sum = cols_sum + got[d, 32:40]
+        cols_sum = cols_sum + spans[d]
     norm = inverse(cols_sum)
     first = jnp.zeros((8, 128), f32)
     second = jnp.zeros((8, 128), f32)
     for d in range(D):
-        weight = got[d, 32:40] * norm
-        first = first + got[d, 0:8] * weight
-        second = second + got[d, 8:16] * weight
+        weight = spans[d] * norm
+        piece = got[d, 0:16].astype(f32)
+        if last:
+            piece = piece + got[d, 16:32].astype(f32)
+        first = first + piece[0:8] * weight
+        second = second + piece[8:16] * weight
     carried = jnp.concatenate([first, second], axis=0)
     sigma = (held[...] * norm)[:, 0:1]
     if not last:
@@ -380,7 +429,7 @@
             ]
 
     sweep(A, table, units, cnt, work)
-    scatter_rows(pay, acc, A, H)
+    scatter_rows(pay, acc, A, H, exact=t_at is not None)
     if t_at is None:
         pred = got[0, 0:16]
         for s in range(1, A):
@@ -398,12 +447,14 @@
         emission = emx[8:16]
         rho = scales_in[:, 1:2] * inv
         ratio[...] = put_lanes([(0, rho * scales_in[:, 0:1])])
-    product = tiles(untile(pred) * emission)
+    product = tiles(untile(pred) * emission).astype(bf16)
     wide = jnp.broadcast_to(cols_sum, (8, 128))
     held[...] = wide
+    wide = jnp.concatenate(halves(wide), axis=0)
+    at = 16 if t_at is None else 32
     for d in range(D):
-        pay[d, 16:32] = product
-        pay[d, 32:40] = wide
+        pay[d, at : at + 16] = product
+        pay[d, at + 16 : at + 32] = wide
 
 
 def gather_kernel(A, H, states, RB, got, carried, emx, terms, scales, pay):
@@ -475,6 +526,7 @@
     sm = pl.BlockSpec(memory_space=pltpu.SMEM)
     hbm = pl.BlockSpec(memory_space=pl.ANY)
     kinds = {"v": vm, "s": sm, "h": hbm, "m": vm}
+    spaces = {"m": pltpu.VMEM, "h": pltpu.HBM}
 
     def run(kinds_in, *args):
         return pl.pallas_call(
@@ -482,7 +534,7 @@
             in_specs=[kinds[c] for c in kinds_in],
             out_specs=[kinds[c] for c, _, _ in outs],
             out_shape=[
-                pltpu.VMEM(s, d) if c == "m" else jax.ShapeDtypeStruct(s, d) for c, s, d in outs
+                spaces[c](s, d) if c in spaces else jax.ShapeDtypeStruct(s, d) for c, s, d in outs
             ],
             scratch_shapes=list(scratch),
             compiler_params=pltpu.CompilerParams(
@@ -490,7 +542,7 @@
             ),
         )(
             *[
-                pltpu.with_memory_space_constraint(a, pltpu.VMEM) if c == "m" else a
+                pltpu.with_memory_space_constraint(a, spaces[c]) if c in spaces else a
                 for c, a in zip(kinds_in, args)
             ]
         )
@@ -515,9 +567,17 @@
     over_src = lambda x: lax.all_to_all(x, "src", 0, 0)
     part = functools.partial
 
-    (block,) = call(part(pack_kernel, A, H), [("v", (A, BLOCK_ROWS, 128), bf16)], big=True)(
-        "vvvvvvv", tokens.reshape(TB, 1), word_table, dst_emb, out_emb,
-        log_norm.reshape(-1, 128), beta_end, block_mask,
+    (block,) = call(
+        part(pack_kernel, A, H),
+        [("v", (A, BLOCK_ROWS, 128), bf16)],
+        [
+            VM(word_table.shape, bf16), VM((dst_emb.shape[0] // 128, 128), f32),
+            VM(beta_end.shape, f32), VM(block_mask.shape[::-1], jnp.int32),
+            pltpu.SMEM(tokens.shape, jnp.int32), pltpu.SemaphoreType.DMA((5 + 2 * A,)),
+        ],
+    )(
+        "hhhhhhh", tokens, word_table, dst_emb, out_emb,
+        log_norm.reshape(-1, 128), beta_end, block_mask.T,
     )
     recv = lax.all_to_all(block, "dst", 0, 0, axis_index_groups=groups)
 
@@ -536,7 +596,7 @@
             ("s", (1,), jnp.int32),
         ],
         [
-            VM((RB, BLK), f32), VM((A, 128), jnp.int32),
+            VM((RB, A, BLK), f32), VM((RB, BLK), f32), VM((A, 128), jnp.int32),
             pltpu.SMEM((A, 128), jnp.int32), VM((32, 128), f32), pltpu.SemaphoreType.DMA(()),
         ],
         big=True,
@@ -546,7 +606,7 @@
     pay, share, emx, em_last, w_last = call(
         part(first_back_kernel, A, H),
         [
-            ("v", (D, 24, 128), f32),
+            ("v", (D, 32, 128), bf16),
             ("v", (D, 2, 128), f32),
             ("v", (TB, CH), f32),
             ("v", (A, 8, CH), f32),
@@ -567,7 +627,7 @@
 
     pay, w_two, held = call(
         part(back_kernel, A, H, states, None),
-        [("v", (D, 40, 128), f32), ("v", (A, 8, CH), bf16), ("v", (8, 128), f32)],
+        [("v", (D, 48, 128), bf16), ("v", (A, 8, CH), bf16), ("v", (8, 128), f32)],
         [acc_rows],
         big=True,
     )("vvvssm", got, factor, emx, units, count, table)
@@ -584,7 +644,7 @@
     pay, terms, ratio, held = call(
         part(back_kernel, A, H, states, 0),
         [
-            ("v", (D, 40, 128), f32), ("v", (A, 8, 128), f32),
+            ("v", (D, 64, 128), bf16), ("v", (A, 8, 128), f32),
             ("v", (8, 128), f32), ("v", (8, 128), f32),
         ],
         [acc_rows, VM((A, 8, CH), bf16)],

time: 204 us -> 186 us (0.912)
  Pallas kernels: 32.7 us -> 26.5 us
  local copies, waits for them, and re-layouts: 7.37 us -> 1.29 us
  blocking collectives: 147 us -> 142 us
    pallas_call x10, Pallas kernels: 32.7 us -> 26.5 us  [run(): pl.pallas_call(body, in_specs=[kinds[c] for c in kinds_in], out_specs=[ki...]
    unnamed x15 -> x4, local copies, waits for them, and re-layouts: 6.62 us -> 1.29 us
    all_to_all x3, blocking collectives: 44.5 us -> 41 us  [local(): over_src = lambda x: lax.all_to_all(x, 'src', 0, 0)]
where the time goes in v3:
time: 186 us
  blocking collectives  142 us (76%)
  Pallas kernels  26.5 us (14%)
  waiting for transfers between devices  10.6 us (6%)
  starting transfers between devices  4.44 us (2%)
    all_to_all x5, blocking collectives, local(): over_dst = lambda x: lax.all_to_all(x, 'dst', 0, 0)  80.2 us
    all_to_all x3, blocking collectives, local(): over_src = lambda x: lax.all_to_all(x, 'src', 0, 0)  41 us
    pallas_call x10, Pallas kernels, run(): pl.pallas_call(body, in_specs=[kinds[c] for c in kinds_in], out_specs=[ki...  26.5 us
    all_to_all x1, blocking collectives, local(): recv = lax.all_to_all(block, 'dst', 0, 0, axis_index_groups=groups)  21.2 us
    ppermute x1, waiting for transfers between devices, local(): alpha_end = lax.ppermute(alpha_end, ('src', 'dst'), swaps)  10.6 us
    ppermute x1, starting transfers between devices, local(): alpha_end = lax.ppermute(alpha_end, ('src', 'dst'), swaps)  4.44 us
  transfers between devices with their start and end apart: 1, of which 1 were waited for; matrix products, arithmetic and copies ran while one was open for 0% of the time, Pallas kernels for 0%

profile of v3, /device:TPU:31, one launch (start us, length us, event | category | flops | bytes accessed | tf_op | source)
XLA Modules:
  0.0 185.9 jit_solution(8289616693671710296)
XLA Ops:
  0.6 1.5 shard_map.112
  2.1 21.2 %all_to_all.45.recv = bf16[8,608,128]{2,1,0:T(8,128)(2,1)} all-to-all(bf16[8,608,128]{2,1,0:T(8,128)(2,1)S(1)} %shard_map.112), channel_id=1, replica_groups={{0,4,8,12,16,20,24,28},{1,5,9,13,17,21,25,29},{2,6,10,14,18,22,26,30},{..., dimensions={0} | all-to-all | bytes 2490368 | tf_op jit(solution)/shard_map/all_to_all | solution.py:582
  23.3 6.6 %shard_map.113 = (bf16[128,256,512]{2,1,0:T(8,128)(2,1)S(1)}, f32[16,8,512]{2,1,0:T(8,128)S(1)}, f32[16,512]{1,0:T(8,128)S(1)}, f32[32,8,128]{2,1,0:T(8,128)S(1)}, s32[128]{0:T(128)S(1)}, /*index=5*/s32[1]{0:T(128)}) custom-call(bf16[8,608,128]{2,1,0:T(8,128)(2,1)} %all_to_all.45.recv, bf16[8192,128]{1,0:T(8,128)(2,1)} %src.1), custom_call_target="tpu_custom_call" | custom-call | tf_op jit(solution)/shard_map/pallas_call | solution.py:532
  29.9 15.0 %all_to_all.46.got = f32[32,8,128]{2,1,0:T(8,128)S(1)} all-to-all(f32[32,8,128]{2,1,0:T(8,128)S(1)} %get-tuple-element.33), channel_id=1, replica_groups=mesh['src'=8,'dst'=32] {'dst'}, dimensions={0} | all-to-all | bytes 262144 | tf_op jit(solution)/shard_map/all_to_all | solution.py:566
  44.9 0.0 copy-start
  44.9 4.1 %shard_map.114 = (bf16[32,32,128]{2,1,0:T(8,128)(2,1)S(1)}, f32[32,2,128]{2,1,0:T(2,128)S(1)}, f32[24,256]{1,0:T(8,128)S(1)}, f32[8,8,256]{2,1,0:T(8,128)S(1)}, bf16[8,8,256]{2,1,0:T(8,128)(2,1)S(1)}) custom-call(f32[32,8,128]{2,1,0:T(8,128)S(1)} %all_to_all.46.got, bf16[8,608,128]{2,1,0:T(8,128)(2,1)} %all_to_all.45.recv, ...), custom_call_target="tpu_custom_call" | custom-call | tf_op jit(solution)/shard_map/pallas_call | solution.py:532
  49.0 13.0 %all_to_all.47.got = bf16[32,32,128]{2,1,0:T(8,128)(2,1)S(1)} all-to-all(bf16[32,32,128]{2,1,0:T(8,128)(2,1)S(1)} %get-tuple-element.39), channel_id=1, replica_groups=mesh['src'=8,'dst'=32] {'dst'}, dimensions={0} | all-to-all | bytes 524288 | tf_op jit(solution)/shard_map/all_to_all | solution.py:566
  62.0 0.0 copy-done
  62.0 2.7 %shard_map.115 = (f32[8,40,128]{2,1,0:T(8,128)S(1)}, f32[16,8,512]{2,1,0:T(8,128)S(1)}) custom-call(bf16[32,32,128]{2,1,0:T(8,128)(2,1)S(1)} %all_to_all.47.got, f32[32,2,128]{2,1,0:T(2,128)S(1)} %get-tuple-element.40.share, f32[8,8192]{1,0:T(8,128)S(1)} %copy-done, f32[16,8,512]{2,1,0:T(8,128)S(1)} %get-tuple-element.34.tops, ...), custom_call_target="tpu_custom_call" | custom-call | tf_op jit(solution)/shard_map/pallas_call | solution.py:532
  64.7 19.1 %all_to_all.48.got = f32[8,40,128]{2,1,0:T(8,128)S(1)} all-to-all(f32[8,40,128]{2,1,0:T(8,128)S(1)} %get-tuple-element.42), channel_id=1, replica_groups=mesh['src'=8,'dst'=32] {'src'}, dimensions={0} | all-to-all | bytes 327680 | tf_op jit(solution)/shard_map/all_to_all | solution.py:567
  83.8 2.1 %shard_map.116 = (bf16[32,48,128]{2,1,0:T(8,128)(2,1)S(1)}, bf16[8,8,256]{2,1,0:T(8,128)(2,1)S(1)}, f32[8,128]{1,0:T(8,128)S(1)}) custom-call(f32[8,40,128]{2,1,0:T(8,128)S(1)} %all_to_all.48.got, f32[16,8,512]{2,1,0:T(8,128)S(1)} %get-tuple-element.43.factor, f32[24,256]{1,0:T(8,128)S(1)} %get-tuple-element.41.emx.em, s32[128]{0:T(128)S(1)} %get-tuple-element.36.units, ...), custom_call_target="tpu_custom_call" | custom-call | tf_op jit(solution)/shard_map/pallas_call | solution.py:532
  86.0 15.3 %all_to_all.49.got = bf16[32,48,128]{2,1,0:T(8,128)(2,1)S(1)} all-to-all(bf16[32,48,128]{2,1,0:T(8,128)(2,1)S(1)} %get-tuple-element.44), channel_id=1, replica_groups=mesh['src'=8,'dst'=32] {'dst'}, dimensions={0} | all-to-all | bytes 786432 | tf_op jit(solution)/shard_map/all_to_all | solution.py:566
  101.3 3.0 %shard_map.117 = (f32[8,40,128]{2,1,0:T(8,128)S(1)}, f32[8,8,128]{2,1,0:T(8,128)S(1)}, f32[8,128]{1,0:T(8,128)S(1)}) custom-call(bf16[32,48,128]{2,1,0:T(8,128)(2,1)S(1)} %all_to_all.49.got, f32[16,8,512]{2,1,0:T(8,128)S(1)} %get-tuple-element.43.factor, bf16[8,8,256]{2,1,0:T(8,128)(2,1)S(1)} %get-tuple-element.45.w_other, ...), custom_call_target="tpu_custom_call" | custom-call | tf_op jit(solution)/shard_map/pallas_call | solution.py:532
  104.3 12.1 %all_to_all.50.got = f32[8,40,128]{2,1,0:T(8,128)S(1)} all-to-all(f32[8,40,128]{2,1,0:T(8,128)S(1)} %get-tuple-element.47), channel_id=1, replica_groups=mesh['src'=8,'dst'=32] {'src'}, dimensions={0} | all-to-all | bytes 327680 | tf_op jit(solution)/shard_map/all_to_all | solution.py:567
  116.4 2.4 %shard_map.118 = (bf16[32,64,128]{2,1,0:T(8,128)(2,1)S(1)}, f32[8,8,128]{2,1,0:T(8,128)S(1)}, f32[8,128]{1,0:T(8,128)S(1)}, f32[8,128]{1,0:T(8,128)S(1)}) custom-call(f32[8,40,128]{2,1,0:T(8,128)S(1)} %all_to_all.50.got, f32[16,8,512]{2,1,0:T(8,128)S(1)} %get-tuple-element.43.factor, f32[24,256]{1,0:T(8,128)S(1)} %get-tuple-element.41.emx.em, ...), custom_call_target="tpu_custom_call" | custom-call | tf_op jit(solution)/shard_map/pallas_call | solution.py:532
  118.7 17.8 %all_to_all.51.got = bf16[32,64,128]{2,1,0:T(8,128)(2,1)S(1)} all-to-all(bf16[32,64,128]{2,1,0:T(8,128)(2,1)S(1)} %get-tuple-element.50), channel_id=1, replica_groups=mesh['src'=8,'dst'=32] {'dst'}, dimensions={0} | all-to-all | bytes 1048576 | tf_op jit(solution)/shard_map/all_to_all | solution.py:566
  136.5 3.0 %shard_map.119 = (f32[8,24,128]{2,1,0:T(8,128)S(1)}, f32[8,8,128]{2,1,0:T(8,128)S(1)}, f32[16,128]{1,0:T(8,128)S(1)}, f32[8,128]{1,0:T(8,128)S(1)}) custom-call(bf16[32,64,128]{2,1,0:T(8,128)(2,1)S(1)} %all_to_all.51.got, f32[16,8,512]{2,1,0:T(8,128)S(1)} %get-tuple-element.43.factor, bf16[8,8,256]{2,1,0:T(8,128)(2,1)S(1)} %get-tuple-element.51.w_other, ...), custom_call_target="tpu_custom_call" | custom-call | tf_op jit(solution)/shard_map/pallas_call | solution.py:532
  139.5 9.9 %all_to_all.52.got = f32[8,24,128]{2,1,0:T(8,128)S(1)} all-to-all(f32[8,24,128]{2,1,0:T(8,128)S(1)} %get-tuple-element.56), channel_id=1, replica_groups=mesh['src'=8,'dst'=32] {'src'}, dimensions={0} | all-to-all | bytes 196608 | tf_op jit(solution)/shard_map/all_to_all | solution.py:567
  149.3 0.2 shard_map.120
  149.5 19.2 %all_to_all.53.got = f32[32,40,128]{2,1,0:T(8,128)S(1)} all-to-all(f32[32,40,128]{2,1,0:T(8,128)S(1)} %shard_map.120), channel_id=1, replica_groups=mesh['src'=8,'dst'=32] {'dst'}, dimensions={0} | all-to-all | bytes 1310720 | tf_op jit(solution)/shard_map/all_to_all | solution.py:566
  168.7 0.9 shard_map.121
  169.6 4.4 %collective-permute-start = (f32[8,2048]{1,0:T(8,128)S(1)}, f32[8,2048]{1,0:T(8,128)S(1)}, u32[]{:S(2)}, u32[]{:S(2)}) collective-permute-start(f32[8,2048]{1,0:T(8,128)S(1)} %get-tuple-element.60), channel_id=1, source_target_pairs={{0,0},{1,1},{2,2},{3,3},{4,32},{5,33},{6,34},{7,35},{8,64},{9,65},... | collective-permute-start | bytes 196616 | tf_op jit(solution)/shard_map/ppermute | solution.py:682
  174.0 0.7 copy.12
  174.7 10.6 %collective-permute-done = f32[8,2048]{1,0:T(8,128)S(1)} collective-permute-done((f32[8,2048]{1,0:T(8,128)S(1)}, f32[8,2048]{1,0:T(8,128)S(1)}, u32[]{:S(2)}, u32[]{:S(2)}) %collective-permute-start) | collective-permute-done | bytes 65568 | tf_op jit(solution)/shard_map/ppermute | solution.py:682
  185.3 0.6 copy.14
Async XLA Ops:
  44.9 17.1 %copy-start = (f32[8,8192]{1,0:T(8,128)S(1)}, f32[8,8192]{1,0:T(8,128)}, u32[]{:S(2)}) copy-start(f32[8,8192]{1,0:T(8,128)} %rest_0_.1) | copy-start | bytes 786436
  169.6 15.7 %collective-permute-start = (f32[8,2048]{1,0:T(8,128)S(1)}, f32[8,2048]{1,0:T(8,128)S(1)}, u32[]{:S(2)}, u32[]{:S(2)}) collective-permute-start(f32[8,2048]{1,0:T(8,128)S(1)} %get-tuple-element.60), channel_id=1, source_target_pairs={{0,0},{1,1},{2,2},{3,3},{4,32},{5,33},{6,34},{7,35},{8,64},{9,65},... | collective-permute-start | bytes 196616 | tf_op jit(solution)/shard_map/ppermute | solution.py:682

commit v4 on v3

--- a/solution.py
+++ b/solution.py
@@ -13,6 +13,7 @@
 TRACES = 8
 TB = STEPS * TRACES
 UNROLL = 8
+LARGE = 24
 TABLE_UNROLL = 4
 very_negative = -1e30
 VMEM_LIMIT = int(20.5 * 1024 * 1024)
@@ -45,6 +46,15 @@
     out = jnp.zeros((8, 128), f32)
     for at, value in pairs:
         out = jnp.where(lane == at, value, out)
+    return out
+
+
+def place_lanes(pieces, width):
+    lane = lanes()
+    out = jnp.zeros((8, 128), f32)
+    for tile, there, here in pieces:
+        moved = tile if there == here else pltpu.roll(tile, (here - there) % 128, 1)
+        out = jnp.where((lane >= here) & (lane < here + width), moved, out)
     return out
 
 
@@ -111,9 +121,11 @@
 
 
 def table_kernel(
-    A, H, recv, src, table, tops, best, pay, units, count,
-    sums, mass, mask_v, mask_s, word_v, mask_sem,
+    A, H, recv, src_h, table, tops, best, pay, units, count,
+    src, src_sem, sums, mass, mask_v, mask_s, word_v, mask_sem,
 ):
+    src_copy = pltpu.make_async_copy(src_h, src, src_sem)
+    src_copy.start()
     RB = src.shape[0] // BLK
     for k in range(A):
         misc = recv[k, MISC_AT : MISC_AT + 16].astype(f32)
@@ -136,6 +148,7 @@
 
     cnt = lax.fori_loop(0, RB, listing, 0)
     count[0] = cnt
+    src_copy.wait()
 
     def some(it, carry):
         for q in range(TABLE_UNROLL):
@@ -179,21 +192,31 @@
 
 
 def sweep(A, table, units, cnt, unit_work):
-    def some(it, carry):
-        base = it * UNROLL
+    def group(base, size, whole):
         results = []
-        for q in range(UNROLL):
-            n = jnp.minimum(base + q, cnt - 1)
+        for q in range(size):
+            n = base + q if whole else jnp.minimum(base + q, cnt - 1)
             u = units[n]
             i = u // A
             k = u - i * A
-            results.append((i, k, base + q < cnt, unit_work(table[n], i, k)))
-        for i, k, valid, (adds) in results:
+            results.append((base + q < cnt, unit_work(table[n], i, k)))
+        for valid, adds in results:
             for ref, index, value in adds:
-                ref[index] += jnp.where(valid, value, 0.0)
+                ref[index] += value if whole else jnp.where(valid, value, 0.0)
+
+    def large(it, carry):
+        group(it * LARGE, LARGE, True)
         return carry
 
-    lax.fori_loop(0, (cnt + UNROLL - 1) // UNROLL, some, 0)
+    whole = cnt // LARGE
+    lax.fori_loop(0, whole, large, 0)
+    done = whole * LARGE
+
+    def small(it, carry):
+        group(done + it * UNROLL, UNROLL, False)
+        return carry
+
+    lax.fori_loop(0, (cnt - done + UNROLL - 1) // UNROLL, small, 0)
 
 
 def backward_unit(weights, factor, acc):
@@ -223,7 +246,7 @@
 
 def first_back_kernel(
     A, H, got, recv, tops, best, units, count, table,
-    pay, share, emx, em_last, w_last, acc, word_v,
+    pay, share, emx, em_last, w_last, acc, word_v, em_all,
 ):
     cnt = count[0]
     D = A * H
@@ -256,11 +279,8 @@
         beta = untile(parts[0:16] + parts[16:32] + parts[32:48])
         em_last[k] = em[16:24]
         w_last[k] = (em[16:24] * beta).astype(bf16)
-
-        @pl.when(mine == k)
-        def _():
-            emx[...] = em
-
+        em_all[k] = em
+    emx[...] = em_all[mine]
     acc[...] = jnp.zeros(acc.shape, f32)
 
     def factor(i, k):
@@ -275,7 +295,7 @@
 
 def send_weights(pay, carried, emission, A):
     whole = jnp.sum(carried[0:8] + carried[8:16], axis=1, keepdims=True)
-    scaled = tiles(emission * (untile(carried) * inverse(whole)))
+    scaled = tiles(emission * (untile(carried) * inverse(whole))).astype(bf16)
     for k in range(A):
         pay[k, 16:32] = scaled
     return whole
@@ -305,7 +325,7 @@
 
     sweep(A, table, units, cnt, work)
     for k in range(A):
-        pay[k, 0:16] = tiles(acc[k])
+        pay[k, 0:16] = tiles(acc[k]).astype(pay.dtype)
     first = jnp.zeros((8, 128), f32)
     second = jnp.zeros((8, 128), f32)
     for d in range(D):
@@ -314,11 +334,11 @@
         second = second + piece[8:16] * share[d, 1:2]
     whole = send_weights(pay, jnp.concatenate([first, second], axis=0), emx[8:16], A)
     for k in range(A):
-        pay[k, 32:40] = put_lanes([(0, whole)])
+        pay[k, 32:48] = jnp.concatenate(halves(put_lanes([(0, whole)])), axis=0)
 
 
 def forward_kernel(
-    A, H, t_at, last, got, factor, w_other, em, held, units, count, table, *rest
+    A, H, states, t_at, last, got, factor, w_other, em, held, units, count, table, *rest
 ):
     if last:
         em_last, terms_in, pay, terms, carried_out, scales, acc, alpha = rest
@@ -348,8 +368,9 @@
         return [(acc, k, pred), (terms, k, jnp.where(lane == t_at * RB + i, term, 0.0))]
 
     sweep(A, table, units, cnt, work)
-    for k in range(A):
-        pay[k, 0:16] = tiles(acc[k])
+    if not last:
+        for k in range(A):
+            pay[k, 0:16] = tiles(acc[k]).astype(pay.dtype)
     spans = [got[d, at + 16 : at + 32].astype(f32) for d in range(D)]
     spans = [x[0:8] + x[8:16] for x in spans]
     cols_sum = spans[0]
@@ -370,16 +391,30 @@
     if not last:
         whole = send_weights(pay, carried, em[0:8], A)
         for k in range(A):
-            pay[k, 32:40] = put_lanes([(0, whole), (1, rows_sum)])
+            pay[k, 32:48] = jnp.concatenate(halves(put_lanes([(0, whole), (1, rows_sum)])), axis=0)
         scales[...] = put_lanes([(0, sigma), (1, rows_sum)])
         return
     carried_out[...] = carried
+    products = []
     reach = jnp.zeros((8, 128), f32)
     every = jnp.zeros((8, 128), f32)
     for k in range(A):
-        product = acc[k] * em_last[k]
+        product = (acc[k] * states) * em_last[k]
+        products.append((product[:, :128], product[:, 128:]))
         reach = reach + (product[:, :128] + product[:, 128:])
         every = every + terms[k]
+    width = CH // A
+    for s in range(A):
+        at = s * width
+        for t in range(2):
+            pay[s, t * 8 : t * 8 + 8] = place_lanes(
+                [
+                    (products[b][at // 128], at % 128, b * width % 128)
+                    for b in range(A)
+                    if b * width // 128 == t
+                ],
+                width,
+            )
     reach = jnp.sum(reach, axis=1, keepdims=True)
     whole = jnp.sum(first + second, axis=1, keepdims=True)
     ratio_one = em[:, 0:1]
@@ -405,12 +440,16 @@
     cnt = count[0]
     D = A * H
     RB = factor.shape[0]
-    cols_sum = got[0, 32:40, 0:1]
+    spans = [got[k, 32:48].astype(f32) for k in range(A)]
+    spans = [x[0:8] + x[8:16] for x in spans]
+    total = spans[0]
     for k in range(1, A):
-        cols_sum = cols_sum + got[k, 32:40, 0:1]
+        total = total + spans[k]
+    cols_sum = total[:, 0:1]
     norm = inverse(cols_sum)
     for k in range(A):
-        weights[k] = (untile(got[k, 16:32]) * (got[k, 32:40, 0:1] * norm)).astype(bf16)
+        share = spans[k][:, 0:1] * norm
+        weights[k] = (untile(got[k, 16:32].astype(f32)) * share).astype(bf16)
     acc[...] = jnp.zeros(acc.shape, f32)
     if t_at is None:
         work = backward_unit(weights, lambda i, k: factor[i, pl.ds(k, 1)], acc)
@@ -431,19 +470,16 @@
     sweep(A, table, units, cnt, work)
     scatter_rows(pay, acc, A, H, exact=t_at is not None)
     if t_at is None:
-        pred = got[0, 0:16]
+        pred = got[0, 0:16].astype(f32)
         for s in range(1, A):
-            pred = pred + got[s, 0:16]
+            pred = pred + got[s, 0:16].astype(f32)
         emission = emx[0:8]
     else:
-        rows_sum = got[0, 32:40, 1:2]
-        for s in range(1, A):
-            rows_sum = rows_sum + got[s, 32:40, 1:2]
-        inv = inverse(rows_sum)
+        inv = inverse(total[:, 1:2])
         pred = jnp.zeros((16, 128), f32)
         for s in range(A):
-            weight = got[s, 32:40, 1:2] * inv * states
-            pred = pred + got[s, 0:16] * jnp.concatenate([weight, weight], axis=0)
+            weight = spans[s][:, 1:2] * inv * states
+            pred = pred + got[s, 0:16].astype(f32) * jnp.concatenate([weight, weight], axis=0)
         emission = emx[8:16]
         rho = scales_in[:, 1:2] * inv
         ratio[...] = put_lanes([(0, rho * scales_in[:, 0:1])])
@@ -457,7 +493,7 @@
         pay[d, at + 16 : at + 32] = wide
 
 
-def gather_kernel(A, H, states, RB, got, carried, emx, terms, scales, pay):
+def gather_kernel(A, H, RB, got, carried, terms, scales, pay):
     rows_sum = got[0, 16:24, 0:1]
     for s in range(1, A):
         rows_sum = rows_sum + got[s, 16:24, 0:1]
@@ -467,40 +503,59 @@
     lane = lanes()
     for s in range(A):
         share = got[s, 16:24, 0:1] * inv
-        weight = share * states
-        pred = pred + got[s, 0:16] * jnp.concatenate([weight, weight], axis=0)
+        pred = pred + got[s, 0:16] * jnp.concatenate([share, share], axis=0)
         piece = got[s, 16:24]
-        piece = jnp.where(lane == 1, piece * weight, piece)
-        piece = jnp.where(lane == 5, piece * share, piece)
+        piece = jnp.where((lane == 1) | (lane == 5), piece * share, piece)
         tail = tail + piece
-    product = tiles(untile(pred) * emx[16:24])
     tail = jnp.where(lane < 6, tail, 0.0)
     tail = jnp.concatenate([tail[:, 64:], tail[:, :64]], axis=1)
     sigma = scales[:, 0:1]
     one = scales[:, 1:2]
     rho = scales[:, 2:3] * inv
     mult = jnp.where(lane < RB, sigma, jnp.where(lane < 2 * RB, one, jnp.where(lane < 3 * RB, rho, 0.0)))
+    width = CH // A
+    row, at = alpha_spot(A)
     for k in range(A):
         last = jnp.where(lane < 3 * RB, terms[k] * mult, 0.0) + tail
+        there = k * width
+        piece = pred[there // 128 * 8 : there // 128 * 8 + 8]
+        piece = place_lanes([(piece, there % 128, at)], width)
         for h in range(H):
-            pay[k * H + h, 32:40] = last
+            if row == 16:
+                pay[k * H + h, 16:24] = last + piece
+            else:
+                pay[k * H + h, 16:24] = last
+                pay[k * H + h, row : row + 8] = piece
     back = carried[...]
     for d in range(A * H):
         pay[d, 0:16] = back
-        pay[d, 16:32] = product
-
-
-def finish_kernel(A, H, states, scale, RB, got, alpha, beta, counts):
-    D = A * H
+
+
+def alpha_spot(A):
+    width = CH // A
+    return (16, 128 - width) if width <= 32 else (24, 0)
+
+
+def spread_kernel(A, H, got, pay):
+    mine = lax.rem(lax.axis_index("dst"), H)
+    width = CH // A
+    row, at = alpha_spot(A)
+    pieces = [got[a * H + mine, row : row + 8] for a in range(A)]
+    for t in range(2):
+        tile = place_lanes(
+            [(pieces[a], at, a * width % 128) for a in range(A) if a * width // 128 == t], width
+        )
+        for s in range(A):
+            pay[s, t * 8 : t * 8 + 8] = tile
+
+
+def finish_kernel(A, H, states, scale, RB, got, sums, alpha, beta, counts):
     lane = lanes()
-    total = got[0, 32:40]
-    for d in range(1, D):
-        total = total + got[d, 32:40]
-    total = jnp.where(lane >= 64, total, 0.0)
-    reach = total[:, 65:66]
-    whole = total[:, 66:67]
-    for_beta = states / whole
-    for_alpha = states / reach
+    total = got[0, 16:24]
+    for d in range(1, A * H):
+        total = total + got[d, 16:24]
+    for_alpha = states / total[:, 65:66]
+    for_beta = states / total[:, 66:67]
     inv = jnp.zeros((8, 128), f32)
     for t in range(STEPS):
         here = (lane >= t * RB) & (lane < (t + 1) * RB)
@@ -508,25 +563,32 @@
     for p in range(2 * RB):
         beta[:, p * CH : (p + 1) * CH] = untile(got[place_of(p, A, H), 0:16]) * for_beta
     mine = lax.rem(lax.axis_index("dst"), H)
-    row = lax.broadcasted_iota(jnp.int32, (RB, 128), 0)
-    wide = lanes((RB, 128))
-    picks = (wide == row) | (wide == row + RB) | (wide == row + 2 * RB)
-    out = jnp.zeros((RB, 128), f32)
+    width = CH // A
+    rows = [jnp.zeros((1, 128), f32) for _ in range(counts.shape[0])]
     for l in range(A):
-        alpha[:, l * CH : (l + 1) * CH] = untile(got[l * H + mine, 16:32]) * for_alpha
-        line = jnp.where(lane < 3 * RB, got[l * H + mine, 32:40] * inv, 0.0)
-        line = jnp.sum(line, axis=0, keepdims=True)
-        column = jnp.sum(jnp.where(picks, line, 0.0), axis=1, keepdims=True)
-        out = out + jnp.where(wide == l // 2, column, 0.0)
-    counts[...] = out[:, : counts.shape[1]]
+        there = l * width
+        for half in range(2):
+            value = place_lanes(
+                [
+                    (sums[s, there // 128 * 8 : there // 128 * 8 + 8], there % 128, s * width % 128)
+                    for s in range(A)
+                    if s * width // 128 == half
+                ],
+                width,
+            )
+            alpha[:, l * CH + half * 128 : l * CH + half * 128 + 128] = value * for_alpha
+        line = jnp.where(lane < 3 * RB, got[l * H + mine, 16:24] * inv, 0.0)
+        rows[l // 2] = rows[l // 2] + jnp.sum(line, axis=0, keepdims=True)
+    out = jnp.concatenate(rows, axis=0)
+    counts[...] = out[:, 0:RB] + out[:, RB : 2 * RB] + out[:, 2 * RB : 3 * RB]
 
 
 def call(body, outs, scratch=(), big=False):
     vm = pl.BlockSpec(memory_space=pltpu.VMEM)
     sm = pl.BlockSpec(memory_space=pltpu.SMEM)
     hbm = pl.BlockSpec(memory_space=pl.ANY)
-    kinds = {"v": vm, "s": sm, "h": hbm, "m": vm}
-    spaces = {"m": pltpu.VMEM, "h": pltpu.HBM}
+    kinds = {"v": vm, "s": sm, "h": hbm, "m": vm, "o": vm}
+    spaces = {"m": pltpu.VMEM, "h": pltpu.HBM, "o": pltpu.HBM}
 
     def run(kinds_in, *args):
         return pl.pallas_call(
@@ -596,11 +658,12 @@
             ("s", (1,), jnp.int32),
         ],
         [
+            VM(src_emb.shape, bf16), pltpu.SemaphoreType.DMA(()),
             VM((RB, A, BLK), f32), VM((RB, BLK), f32), VM((A, 128), jnp.int32),
             pltpu.SMEM((A, 128), jnp.int32), VM((32, 128), f32), pltpu.SemaphoreType.DMA(()),
         ],
         big=True,
-    )("vv", recv, src_emb)
+    )("vh", recv, src_emb)
     got = over_dst(pay)
 
     pay, share, emx, em_last, w_last = call(
@@ -612,14 +675,14 @@
             ("v", (A, 8, CH), f32),
             ("v", (A, 8, CH), bf16),
         ],
-        [acc_rows, VM((TB, 128), f32)],
+        [acc_rows, VM((TB, 128), f32), VM((A, TB, CH), f32)],
         big=True,
     )("vvvvssm", got, recv, tops, best, units, count, table)
     got = over_dst(pay)
 
     pay, factor = call(
         part(first_forward_kernel, A, H),
-        [("v", (A, 40, 128), f32), ("v", (RB, A, BLK), f32)],
+        [("v", (A, 48, 128), bf16), ("v", (RB, A, BLK), f32)],
         [acc_cols],
         big=True,
     )("vvvvvssm", got, share, alpha_start, tops, emx, units, count, table)
@@ -634,8 +697,8 @@
     got = over_dst(pay)
 
     pay, terms, scales = call(
-        part(forward_kernel, A, H, 1, False),
-        [("v", (A, 40, 128), f32), ("v", (A, 8, 128), f32), ("v", (8, 128), f32)],
+        part(forward_kernel, A, H, states, 1, False),
+        [("v", (A, 48, 128), bf16), ("v", (A, 8, 128), f32), ("v", (8, 128), f32)],
         [acc_cols, acc_rows],
         big=True,
     )("vvvvvssm", got, factor, w_two, emx, held, units, count, table)
@@ -653,7 +716,7 @@
     got = over_dst(pay)
 
     pay, terms, carried, scales = call(
-        part(forward_kernel, A, H, 2, True),
+        part(forward_kernel, A, H, states, 2, True),
         [
             ("v", (A, 24, 128), f32), ("v", (A, 8, 128), f32),
             ("v", (16, 128), f32), ("v", (8, 128), f32),
@@ -663,24 +726,23 @@
     )("vvvvvssmvv", got, factor, w_last, ratio, held, units, count, table, em_last, terms)
     got = over_src(pay)
 
-    (pay,) = call(part(gather_kernel, A, H, states, RB), [("v", (D, 40, 128), f32)])(
-        "vvvvv", got, carried, emx, terms, scales
-    )
+    (pay,) = call(
+        part(gather_kernel, A, H, RB), [("v", (D, alpha_spot(A)[0] // 8 * 8 + 8, 128), f32)]
+    )("vvvv", got, carried, terms, scales)
     got = over_dst(pay)
+
+    (pay,) = call(part(spread_kernel, A, H), [("v", (A, 16, 128), f32)])("v", got)
+    sums = over_src(pay)
 
     alpha_end, beta_start, counts = call(
         part(finish_kernel, A, H, states, NB * NB / TB, RB),
         [
-            ("v", (8, A * CH), f32),
-            ("v", (8, rows), f32),
-            ("v", (RB, block_mask.shape[1]), f32),
+            ("o", (8, A * CH), f32),
+            ("o", (8, rows), f32),
+            ("o", (block_mask.shape[1], RB), f32),
         ],
-    )("v", got)
-    swaps = [
-        (a * D + b * H + h, b * D + a * H + h) for a in range(A) for b in range(A) for h in range(H)
-    ]
-    alpha_end = lax.ppermute(alpha_end, ("src", "dst"), swaps)
-    return (alpha_end, beta_start, counts)
+    )("vv", got, sums)
+    return (alpha_end, beta_start, counts.T)
 
 
 def solution(mesh):

time: 186 us -> 176 us (0.946)
  the two profiles are of different devices: /device:TPU:31 before, /device:TPU:1 now
where the time goes in v4:
time: 176 us; the launch traced here: 175 us
  blocking collectives  144 us (82%)
  Pallas kernels  30.5 us (17%)
    all_to_all x5, blocking collectives, local(): over_dst = lambda x: lax.all_to_all(x, 'dst', 0, 0)  70 us
    all_to_all x4, blocking collectives, local(): over_src = lambda x: lax.all_to_all(x, 'src', 0, 0)  49.2 us
    pallas_call x11, Pallas kernels, run(): pl.pallas_call(body, in_specs=[kinds[c] for c in kinds_in], out_specs=[ki...  30.5 us
    all_to_all x1, blocking collectives, local(): recv = lax.all_to_all(block, 'dst', 0, 0, axis_index_groups=groups)  24.9 us

profile of v4, /device:TPU:1, one launch (start us, length us, event | category | flops | bytes accessed | tf_op | source)
XLA Modules:
  0.0 175.4 jit_solution(17602341708414497106)
XLA Ops:
  0.6 1.5 shard_map.112
  2.1 24.9 %all_to_all.50.recv = bf16[8,608,128]{2,1,0:T(8,128)(2,1)} all-to-all(bf16[8,608,128]{2,1,0:T(8,128)(2,1)S(1)} %shard_map.112), channel_id=1, replica_groups={{0,4,8,12,16,20,24,28},{1,5,9,13,17,21,25,29},{2,6,10,14,18,22,26,30},{..., dimensions={0} | all-to-all | bytes 2490368 | tf_op jit(solution)/shard_map/all_to_all | solution.py:644
  27.1 8.0 %shard_map.113 = (bf16[128,256,512]{2,1,0:T(8,128)(2,1)S(1)}, f32[16,8,512]{2,1,0:T(8,128)S(1)}, f32[16,512]{1,0:T(8,128)S(1)}, f32[32,8,128]{2,1,0:T(8,128)S(1)}, s32[128]{0:T(128)S(1)}, /*index=5*/s32[1]{0:T(128)}) custom-call(bf16[8,608,128]{2,1,0:T(8,128)(2,1)} %all_to_all.50.recv, bf16[8192,128]{1,0:T(8,128)(2,1)} %src_h.1), custom_call_target="tpu_custom_call" | custom-call | tf_op jit(solution)/shard_map/pallas_call | solution.py:594
  35.1 13.7 %all_to_all.51.got = f32[32,8,128]{2,1,0:T(8,128)S(1)} all-to-all(f32[32,8,128]{2,1,0:T(8,128)S(1)} %get-tuple-element.33), channel_id=1, replica_groups=mesh['src'=8,'dst'=32] {'dst'}, dimensions={0} | all-to-all | bytes 262144 | tf_op jit(solution)/shard_map/all_to_all | solution.py:628
  48.8 0.0 copy-start
  48.8 3.5 %shard_map.114 = (bf16[32,32,128]{2,1,0:T(8,128)(2,1)S(1)}, f32[32,2,128]{2,1,0:T(2,128)S(1)}, f32[24,256]{1,0:T(8,128)S(1)}, f32[8,8,256]{2,1,0:T(8,128)S(1)}, bf16[8,8,256]{2,1,0:T(8,128)(2,1)S(1)}) custom-call(f32[32,8,128]{2,1,0:T(8,128)S(1)} %all_to_all.51.got, bf16[8,608,128]{2,1,0:T(8,128)(2,1)} %all_to_all.50.recv, ...), custom_call_target="tpu_custom_call" | custom-call | tf_op jit(solution)/shard_map/pallas_call | solution.py:594
  52.4 12.6 %all_to_all.52.got = bf16[32,32,128]{2,1,0:T(8,128)(2,1)S(1)} all-to-all(bf16[32,32,128]{2,1,0:T(8,128)(2,1)S(1)} %get-tuple-element.39), channel_id=1, replica_groups=mesh['src'=8,'dst'=32] {'dst'}, dimensions={0} | all-to-all | bytes 524288 | tf_op jit(solution)/shard_map/all_to_all | solution.py:628
  64.9 0.0 copy-done
  64.9 3.4 %shard_map.115 = (bf16[8,48,128]{2,1,0:T(8,128)(2,1)S(1)}, f32[16,8,512]{2,1,0:T(8,128)S(1)}) custom-call(bf16[32,32,128]{2,1,0:T(8,128)(2,1)S(1)} %all_to_all.52.got, f32[32,2,128]{2,1,0:T(2,128)S(1)} %get-tuple-element.40.share, f32[8,8192]{1,0:T(8,128)S(1)} %copy-done, f32[16,8,512]{2,1,0:T(8,128)S(1)} %get-tuple-element.34.tops, ...), custom_call_target="tpu_custom_call" | custom-call | tf_op jit(solution)/shard_map/pallas_call | solution.py:594
  68.4 16.8 %all_to_all.53.got = bf16[8,48,128]{2,1,0:T(8,128)(2,1)S(1)} all-to-all(bf16[8,48,128]{2,1,0:T(8,128)(2,1)S(1)} %get-tuple-element.42), channel_id=1, replica_groups=mesh['src'=8,'dst'=32] {'src'}, dimensions={0} | all-to-all | bytes 196608 | tf_op jit(solution)/shard_map/all_to_all | solution.py:629
  85.1 2.5 %shard_map.116 = (bf16[32,48,128]{2,1,0:T(8,128)(2,1)S(1)}, bf16[8,8,256]{2,1,0:T(8,128)(2,1)S(1)}, f32[8,128]{1,0:T(8,128)S(1)}) custom-call(bf16[8,48,128]{2,1,0:T(8,128)(2,1)S(1)} %all_to_all.53.got, f32[16,8,512]{2,1,0:T(8,128)S(1)} %get-tuple-element.43.factor, f32[24,256]{1,0:T(8,128)S(1)} %get-tuple-element.41.emx.em, ...), custom_call_target="tpu_custom_call" | custom-call | tf_op jit(solution)/shard_map/pallas_call | solution.py:594
  87.7 14.8 %all_to_all.54.got = bf16[32,48,128]{2,1,0:T(8,128)(2,1)S(1)} all-to-all(bf16[32,48,128]{2,1,0:T(8,128)(2,1)S(1)} %get-tuple-element.44), channel_id=1, replica_groups=mesh['src'=8,'dst'=32] {'dst'}, dimensions={0} | all-to-all | bytes 786432 | tf_op jit(solution)/shard_map/all_to_all | solution.py:628
  102.5 3.7 %shard_map.117 = (bf16[8,48,128]{2,1,0:T(8,128)(2,1)S(1)}, f32[8,8,128]{2,1,0:T(8,128)S(1)}, f32[8,128]{1,0:T(8,128)S(1)}) custom-call(bf16[32,48,128]{2,1,0:T(8,128)(2,1)S(1)} %all_to_all.54.got, f32[16,8,512]{2,1,0:T(8,128)S(1)} %get-tuple-element.43.factor, bf16[8,8,256]{2,1,0:T(8,128)(2,1)S(1)} %get-tuple-element.45.w_other, ...), custom_call_target="tpu_custom_call" | custom-call | tf_op jit(solution)/shard_map/pallas_call | solution.py:594
  106.2 11.2 %all_to_all.55.got = bf16[8,48,128]{2,1,0:T(8,128)(2,1)S(1)} all-to-all(bf16[8,48,128]{2,1,0:T(8,128)(2,1)S(1)} %get-tuple-element.47), channel_id=1, replica_groups=mesh['src'=8,'dst'=32] {'src'}, dimensions={0} | all-to-all | bytes 196608 | tf_op jit(solution)/shard_map/all_to_all | solution.py:629
  117.4 2.8 %shard_map.118 = (bf16[32,64,128]{2,1,0:T(8,128)(2,1)S(1)}, f32[8,8,128]{2,1,0:T(8,128)S(1)}, f32[8,128]{1,0:T(8,128)S(1)}, f32[8,128]{1,0:T(8,128)S(1)}) custom-call(bf16[8,48,128]{2,1,0:T(8,128)(2,1)S(1)} %all_to_all.55.got, f32[16,8,512]{2,1,0:T(8,128)S(1)} %get-tuple-element.43.factor, f32[24,256]{1,0:T(8,128)S(1)} %get-tuple-element.41.emx.em, ...), custom_call_target="tpu_custom_call" | custom-call | tf_op jit(solution)/shard_map/pallas_call | solution.py:594
  120.2 15.2 %all_to_all.56.got = bf16[32,64,128]{2,1,0:T(8,128)(2,1)S(1)} all-to-all(bf16[32,64,128]{2,1,0:T(8,128)(2,1)S(1)} %get-tuple-element.50), channel_id=1, replica_groups=mesh['src'=8,'dst'=32] {'dst'}, dimensions={0} | all-to-all | bytes 1048576 | tf_op jit(solution)/shard_map/all_to_all | solution.py:628
  135.5 3.8 %shard_map.119 = (f32[8,24,128]{2,1,0:T(8,128)S(1)}, f32[8,8,128]{2,1,0:T(8,128)S(1)}, f32[16,128]{1,0:T(8,128)S(1)}, f32[8,128]{1,0:T(8,128)S(1)}) custom-call(bf16[32,64,128]{2,1,0:T(8,128)(2,1)S(1)} %all_to_all.56.got, f32[16,8,512]{2,1,0:T(8,128)S(1)} %get-tuple-element.43.factor, bf16[8,8,256]{2,1,0:T(8,128)(2,1)S(1)} %get-tuple-element.51.w_other, ...), custom_call_target="tpu_custom_call" | custom-call | tf_op jit(solution)/shard_map/pallas_call | solution.py:594
  139.2 11.3 %all_to_all.57.got = f32[8,24,128]{2,1,0:T(8,128)S(1)} all-to-all(f32[8,24,128]{2,1,0:T(8,128)S(1)} %get-tuple-element.56), channel_id=1, replica_groups=mesh['src'=8,'dst'=32] {'src'}, dimensions={0} | all-to-all | bytes 196608 | tf_op jit(solution)/shard_map/all_to_all | solution.py:629
  150.5 0.2 shard_map.120
  150.7 13.8 %all_to_all.58.got = f32[32,24,128]{2,1,0:T(8,128)S(1)} all-to-all(f32[32,24,128]{2,1,0:T(8,128)S(1)} %shard_map.120), channel_id=1, replica_groups=mesh['src'=8,'dst'=32] {'dst'}, dimensions={0} | all-to-all | bytes 786432 | tf_op jit(solution)/shard_map/all_to_all | solution.py:628
  164.5 0.1 shard_map.121
  164.5 9.9 %all_to_all.59.sums = f32[8,16,128]{2,1,0:T(8,128)S(1)} all-to-all(f32[8,16,128]{2,1,0:T(8,128)S(1)} %shard_map.121), channel_id=1, replica_groups=mesh['src'=8,'dst'=32] {'src'}, dimensions={0} | all-to-all | bytes 131072 | tf_op jit(solution)/shard_map/all_to_all | solution.py:629
  174.5 0.9 shard_map.122
Async XLA Ops:
  48.8 16.1 %copy-start = (f32[8,8192]{1,0:T(8,128)S(1)}, f32[8,8192]{1,0:T(8,128)}, u32[]{:S(2)}) copy-start(f32[8,8192]{1,0:T(8,128)} %rest_0_.1) | copy-start | bytes 786436

commit v5 on v4

--- a/solution.py
+++ b/solution.py
@@ -12,7 +12,7 @@
 STEPS = 3
 TRACES = 8
 TB = STEPS * TRACES
-UNROLL = 8
+UNROLL = 12
 LARGE = 24
 TABLE_UNROLL = 4
 very_negative = -1e30

time: 176 us -> 176 us (level)
  blocking collectives: 144 us -> 147 us
where the time goes in v5:
time: 176 us
  blocking collectives  147 us (84%)
  Pallas kernels  28.8 us (16%)
    all_to_all x5, blocking collectives, local(): over_dst = lambda x: lax.all_to_all(x, 'dst', 0, 0)  71.6 us
    all_to_all x4, blocking collectives, local(): over_src = lambda x: lax.all_to_all(x, 'src', 0, 0)  50.1 us
    pallas_call x11, Pallas kernels, run(): pl.pallas_call(body, in_specs=[kinds[c] for c in kinds_in], out_specs=[ki...  28.8 us
    all_to_all x1, blocking collectives, local(): recv = lax.all_to_all(block, 'dst', 0, 0, axis_index_groups=groups)  24.9 us

profile of v5, /device:TPU:1, one launch (start us, length us, event | category | flops | bytes accessed | tf_op | source)
XLA Modules:
  0.0 176.1 jit_solution(3310473762137761802)
XLA Ops:
  0.6 1.5 shard_map.112
  2.1 24.9 %all_to_all.50.recv = bf16[8,608,128]{2,1,0:T(8,128)(2,1)} all-to-all(bf16[8,608,128]{2,1,0:T(8,128)(2,1)S(1)} %shard_map.112), channel_id=1, replica_groups={{0,4,8,12,16,20,24,28},{1,5,9,13,17,21,25,29},{2,6,10,14,18,22,26,30},{..., dimensions={0} | all-to-all | bytes 2490368 | tf_op jit(solution)/shard_map/all_to_all | solution.py:644
  27.1 7.3 %shard_map.113 = (bf16[128,256,512]{2,1,0:T(8,128)(2,1)S(1)}, f32[16,8,512]{2,1,0:T(8,128)S(1)}, f32[16,512]{1,0:T(8,128)S(1)}, f32[32,8,128]{2,1,0:T(8,128)S(1)}, s32[128]{0:T(128)S(1)}, /*index=5*/s32[1]{0:T(128)}) custom-call(bf16[8,608,128]{2,1,0:T(8,128)(2,1)} %all_to_all.50.recv, bf16[8192,128]{1,0:T(8,128)(2,1)} %src_h.1), custom_call_target="tpu_custom_call" | custom-call | tf_op jit(solution)/shard_map/pallas_call | solution.py:594
  34.4 13.9 %all_to_all.51.got = f32[32,8,128]{2,1,0:T(8,128)S(1)} all-to-all(f32[32,8,128]{2,1,0:T(8,128)S(1)} %get-tuple-element.33), channel_id=1, replica_groups=mesh['src'=8,'dst'=32] {'dst'}, dimensions={0} | all-to-all | bytes 262144 | tf_op jit(solution)/shard_map/all_to_all | solution.py:628
  48.2 0.0 copy-start
  48.2 3.4 %shard_map.114 = (bf16[32,32,128]{2,1,0:T(8,128)(2,1)S(1)}, f32[32,2,128]{2,1,0:T(2,128)S(1)}, f32[24,256]{1,0:T(8,128)S(1)}, f32[8,8,256]{2,1,0:T(8,128)S(1)}, bf16[8,8,256]{2,1,0:T(8,128)(2,1)S(1)}) custom-call(f32[32,8,128]{2,1,0:T(8,128)S(1)} %all_to_all.51.got, bf16[8,608,128]{2,1,0:T(8,128)(2,1)} %all_to_all.50.recv, ...), custom_call_target="tpu_custom_call" | custom-call | tf_op jit(solution)/shard_map/pallas_call | solution.py:594
  51.6 12.6 %all_to_all.52.got = bf16[32,32,128]{2,1,0:T(8,128)(2,1)S(1)} all-to-all(bf16[32,32,128]{2,1,0:T(8,128)(2,1)S(1)} %get-tuple-element.39), channel_id=1, replica_groups=mesh['src'=8,'dst'=32] {'dst'}, dimensions={0} | all-to-all | bytes 524288 | tf_op jit(solution)/shard_map/all_to_all | solution.py:628
  64.2 0.0 copy-done
  64.2 3.3 %shard_map.115 = (bf16[8,48,128]{2,1,0:T(8,128)(2,1)S(1)}, f32[16,8,512]{2,1,0:T(8,128)S(1)}) custom-call(bf16[32,32,128]{2,1,0:T(8,128)(2,1)S(1)} %all_to_all.52.got, f32[32,2,128]{2,1,0:T(2,128)S(1)} %get-tuple-element.40.share, f32[8,8192]{1,0:T(8,128)S(1)} %copy-done, f32[16,8,512]{2,1,0:T(8,128)S(1)} %get-tuple-element.34.tops, ...), custom_call_target="tpu_custom_call" | custom-call | tf_op jit(solution)/shard_map/pallas_call | solution.py:594
  67.5 18.5 %all_to_all.53.got = bf16[8,48,128]{2,1,0:T(8,128)(2,1)S(1)} all-to-all(bf16[8,48,128]{2,1,0:T(8,128)(2,1)S(1)} %get-tuple-element.42), channel_id=1, replica_groups=mesh['src'=8,'dst'=32] {'src'}, dimensions={0} | all-to-all | bytes 196608 | tf_op jit(solution)/shard_map/all_to_all | solution.py:629
  86.0 2.4 %shard_map.116 = (bf16[32,48,128]{2,1,0:T(8,128)(2,1)S(1)}, bf16[8,8,256]{2,1,0:T(8,128)(2,1)S(1)}, f32[8,128]{1,0:T(8,128)S(1)}) custom-call(bf16[8,48,128]{2,1,0:T(8,128)(2,1)S(1)} %all_to_all.53.got, f32[16,8,512]{2,1,0:T(8,128)S(1)} %get-tuple-element.43.factor, f32[24,256]{1,0:T(8,128)S(1)} %get-tuple-element.41.emx.em, ...), custom_call_target="tpu_custom_call" | custom-call | tf_op jit(solution)/shard_map/pallas_call | solution.py:594
  88.4 14.2 %all_to_all.54.got = bf16[32,48,128]{2,1,0:T(8,128)(2,1)S(1)} all-to-all(bf16[32,48,128]{2,1,0:T(8,128)(2,1)S(1)} %get-tuple-element.44), channel_id=1, replica_groups=mesh['src'=8,'dst'=32] {'dst'}, dimensions={0} | all-to-all | bytes 786432 | tf_op jit(solution)/shard_map/all_to_all | solution.py:628
  102.6 3.6 %shard_map.117 = (bf16[8,48,128]{2,1,0:T(8,128)(2,1)S(1)}, f32[8,8,128]{2,1,0:T(8,128)S(1)}, f32[8,128]{1,0:T(8,128)S(1)}) custom-call(bf16[32,48,128]{2,1,0:T(8,128)(2,1)S(1)} %all_to_all.54.got, f32[16,8,512]{2,1,0:T(8,128)S(1)} %get-tuple-element.43.factor, bf16[8,8,256]{2,1,0:T(8,128)(2,1)S(1)} %get-tuple-element.45.w_other, ...), custom_call_target="tpu_custom_call" | custom-call | tf_op jit(solution)/shard_map/pallas_call | solution.py:594
  106.2 10.6 %all_to_all.55.got = bf16[8,48,128]{2,1,0:T(8,128)(2,1)S(1)} all-to-all(bf16[8,48,128]{2,1,0:T(8,128)(2,1)S(1)} %get-tuple-element.47), channel_id=1, replica_groups=mesh['src'=8,'dst'=32] {'src'}, dimensions={0} | all-to-all | bytes 196608 | tf_op jit(solution)/shard_map/all_to_all | solution.py:629
  116.8 2.6 %shard_map.118 = (bf16[32,64,128]{2,1,0:T(8,128)(2,1)S(1)}, f32[8,8,128]{2,1,0:T(8,128)S(1)}, f32[8,128]{1,0:T(8,128)S(1)}, f32[8,128]{1,0:T(8,128)S(1)}) custom-call(bf16[8,48,128]{2,1,0:T(8,128)(2,1)S(1)} %all_to_all.55.got, f32[16,8,512]{2,1,0:T(8,128)S(1)} %get-tuple-element.43.factor, f32[24,256]{1,0:T(8,128)S(1)} %get-tuple-element.41.emx.em, ...), custom_call_target="tpu_custom_call" | custom-call | tf_op jit(solution)/shard_map/pallas_call | solution.py:594
  119.5 16.4 %all_to_all.56.got = bf16[32,64,128]{2,1,0:T(8,128)(2,1)S(1)} all-to-all(bf16[32,64,128]{2,1,0:T(8,128)(2,1)S(1)} %get-tuple-element.50), channel_id=1, replica_groups=mesh['src'=8,'dst'=32] {'dst'}, dimensions={0} | all-to-all | bytes 1048576 | tf_op jit(solution)/shard_map/all_to_all | solution.py:628
  135.9 3.6 %shard_map.119 = (f32[8,24,128]{2,1,0:T(8,128)S(1)}, f32[8,8,128]{2,1,0:T(8,128)S(1)}, f32[16,128]{1,0:T(8,128)S(1)}, f32[8,128]{1,0:T(8,128)S(1)}) custom-call(bf16[32,64,128]{2,1,0:T(8,128)(2,1)S(1)} %all_to_all.56.got, f32[16,8,512]{2,1,0:T(8,128)S(1)} %get-tuple-element.43.factor, bf16[8,8,256]{2,1,0:T(8,128)(2,1)S(1)} %get-tuple-element.51.w_other, ...), custom_call_target="tpu_custom_call" | custom-call | tf_op jit(solution)/shard_map/pallas_call | solution.py:594
  139.5 11.1 %all_to_all.57.got = f32[8,24,128]{2,1,0:T(8,128)S(1)} all-to-all(f32[8,24,128]{2,1,0:T(8,128)S(1)} %get-tuple-element.56), channel_id=1, replica_groups=mesh['src'=8,'dst'=32] {'src'}, dimensions={0} | all-to-all | bytes 196608 | tf_op jit(solution)/shard_map/all_to_all | solution.py:629
  150.5 0.2 shard_map.120
  150.7 14.5 %all_to_all.58.got = f32[32,24,128]{2,1,0:T(8,128)S(1)} all-to-all(f32[32,24,128]{2,1,0:T(8,128)S(1)} %shard_map.120), channel_id=1, replica_groups=mesh['src'=8,'dst'=32] {'dst'}, dimensions={0} | all-to-all | bytes 786432 | tf_op jit(solution)/shard_map/all_to_all | solution.py:628
  165.2 0.1 shard_map.121
  165.3 9.9 %all_to_all.59.sums = f32[8,16,128]{2,1,0:T(8,128)S(1)} all-to-all(f32[8,16,128]{2,1,0:T(8,128)S(1)} %shard_map.121), channel_id=1, replica_groups=mesh['src'=8,'dst'=32] {'src'}, dimensions={0} | all-to-all | bytes 131072 | tf_op jit(solution)/shard_map/all_to_all | solution.py:629
  175.2 0.9 shard_map.122
Async XLA Ops:
  48.2 16.0 %copy-start = (f32[8,8192]{1,0:T(8,128)S(1)}, f32[8,8192]{1,0:T(8,128)}, u32[]{:S(2)}) copy-start(f32[8,8192]{1,0:T(8,128)} %rest_0_.1) | copy-start | bytes 786436
